TPU v7x, 32 devices: a whole 2x2x4 slice. The times are simulated.
32 devices in a mesh: grp: 2 (over y), space: 4 (over z), cuts: 2 (over x), sub: 2 (over core).
Axes of the slice: x: 2, y: 2, z: 4, core: 2. Of those that a mesh axis runs over, the one named last changes fastest.
Arguments:
- starts: float32 [16, 2, 256, 512], P(('grp', 'cuts'), None, ('space', 'sub')), parts along dimension 0, may hold values from -6 to 6
- coarse_prev: float32 [16, 2, 64, 128], P(('grp', 'cuts'), None, ('space', 'sub')), parts along dimension 0, may hold values from -6 to 6
- zone_ids: int32 [512, 512], P(('grp', 'space', 'sub')), parts along dimension 0, may hold values from 0 to 7
- materials: float32 [4, 8], replicated, may hold values from 0.05 to 0.2
- current: int32 [192], P('grp'), parts along dimension 0, may hold values from 0 to 1999
- bounds: int32 [8], replicated, may hold values from 0 to 94
Outputs:
- ends: float32 [16, 2, 256, 512], P(('grp', 'cuts'), None, ('space', 'sub')), parts along dimension 0
- coarse_new: float32 [16, 2, 64, 128], P(('grp', 'cuts'), None, ('space', 'sub')), parts along dimension 0
There are 2 independent parts, one for each index of `grp`. A program takes and returns all parts, laid end to end along the dimension named above; an argument that names none is the same for every part. Nothing has to cross between parts.
All inputs are finite; a program needn't handle non-finite values.
Results may differ from a plain program's by a relative error of at most 0.0001.
Values sent between devices are 32-bit elements; how exact they have to be, the bound alone decides.
A program may use at most 64 MiB of HBM per device.

v0:
```python
import jax
import jax.numpy as jnp
from jax import lax
from jax.sharding import PartitionSpec as P

FSTEPS = 2


JOULE_GAIN = 0.5


def extended(block, sides, width):
    for axis, dim in sides:
        count = lax.axis_size(axis)
        forward = [(i, i + 1) for i in range(count - 1)]
        backward = [(target, source) for source, target in forward]
        low = lax.ppermute(
            lax.slice_in_dim(block, block.shape[dim] - width, None, axis=dim), axis, forward
        )
        high = lax.ppermute(lax.slice_in_dim(block, 0, width, axis=dim), axis, backward)
        block = jnp.concatenate([low, block, high], axis=dim)
    return block


def shifted(value, axis, steps):
    count = lax.axis_size(axis)
    initial, last = (max(0, -steps), min(count, count - steps))
    return lax.ppermute(value, axis, [(source, source + steps) for source in range(initial, last)])


def restrict(values):
    shape = values.shape
    blocks = values.reshape(shape[:-2] + (shape[-2] // 4, 4, shape[-1] // 4, 4))
    return jnp.mean(blocks, axis=(-3, -1))


def prolong(coarse):
    return jnp.repeat(jnp.repeat(coarse, 4, axis=-2), 4, axis=-1)


def material_fields(zone_pad, materials):
    fields = jnp.zeros((4,) + zone_pad.shape, jnp.float32)
    for zone_no in range(materials.shape[1]):
        present = (zone_pad == zone_no)[None]
        fields = jnp.where(present, materials[:, zone_no][:, None, None], fields)
    return fields


def stencil(padded, diffusion):
    center = padded[:, 1:-1, 1:-1]
    own = diffusion[:, 1:-1, 1:-1]
    summed = 0.5 * (diffusion[:, 2:, 1:-1] + own) * (padded[:, 2:, 1:-1] - center)
    summed = summed + 0.5 * (diffusion[:, :-2, 1:-1] + own) * (padded[:, :-2, 1:-1] - center)
    summed = summed + 0.5 * (diffusion[:, 1:-1, 2:] + own) * (padded[:, 1:-1, 2:] - center)
    summed = summed + 0.5 * (diffusion[:, 1:-1, :-2] + own) * (padded[:, 1:-1, :-2] - center)
    return summed


def advance(padded, diffusion, coupling, turns, amperes, time_span):
    center = padded[:, 1:-1, 1:-1]
    spread = stencil(padded, diffusion)
    change = spread[0] + time_span * turns * amperes
    magnet = center[0] + change
    thermal = center[1] + spread[1] + JOULE_GAIN * change * change
    coupled = time_span * coupling
    diagonal = 1.0 + coupled
    offdiag = 0.5 * coupled
    determinant = diagonal * diagonal - offdiag * offdiag
    return jnp.stack(
        [
            (diagonal * magnet + offdiag * thermal) / determinant,
            (offdiag * magnet + diagonal * thermal) / determinant,
        ]
    )


def pad_columns(values):
    return jnp.pad(values, ((0, 0), (0, 0), (1, 1)))


def coarse_step(state, coarse_diff, coarse_link, coarse_turn, amperes):
    rimmed = extended(state, ((("space", "sub"), 1),), 1)
    return advance(pad_columns(rimmed), coarse_diff, coarse_link, coarse_turn, amperes, 2.0)


def local(starts, coarse_prev, zone_ids, materials, current, bounds):
    local_count = starts.shape[0]
    row_count = zone_ids.shape[0]
    cut_index = lax.axis_index("cuts")
    rimmed_zones = extended(zone_ids, ((("space", "sub"), 0),), 4)
    zone_pad = jnp.pad(rimmed_zones, ((0, 0), (4, 4)))
    fields = material_fields(zone_pad, materials)
    fine_diff = fields[0:2, 3:-3, 3:-3]
    fine_link = fields[2, 4:-4, 4:-4]
    fine_turn = fields[3, 4:-4, 4:-4]
    coarse_fields = restrict(fields)
    coarse_diff = coarse_fields[0:2] * 0.125
    coarse_link = coarse_fields[2, 1:-1, 1:-1]
    coarse_turn = coarse_fields[3, 1:-1, 1:-1]
    amperes_all = current.astype(jnp.float32) * 0.001
    coarse_rows = row_count // 4

    def profile_at(slice_no, offset):
        first_step = lax.dynamic_index_in_dim(bounds, slice_no, 0, False)
        return lax.dynamic_index_in_dim(amperes_all, first_step + offset, 0, False)

    def prepare(stacked):

        def plain_step(state, amperes):
            return coarse_step(state, coarse_diff, coarse_link, coarse_turn, amperes)

        def keep_rows(state):
            return state

        return (stacked, plain_step, keep_rows)

    corrections = []
    restricted = []
    for local_no in range(local_count):
        slice_no = cut_index * local_count + local_no
        state = starts[local_no]
        for step_no in range(FSTEPS):
            rimmed = extended(state, ((("space", "sub"), 1),), 1)
            state = advance(
                pad_columns(rimmed),
                fine_diff,
                fine_link,
                fine_turn,
                profile_at(slice_no, step_no),
                1.0,
            )
        correction = state - prolong(coarse_prev[local_no])
        corrections.append(correction)
        restricted.append(restrict(correction))
    first_coarse = restrict(starts[0])
    column_count = first_coarse.shape[2]
    stacked = jnp.concatenate(
        [first_coarse, jnp.stack(restricted).reshape(2 * local_count, coarse_rows, column_count)],
        axis=0,
    )
    states, stepper, cropper = prepare(stacked)
    first_state = states[0:2]
    cut_count = lax.axis_size("cuts")
    coarse_state = first_state
    coarse_outs = []
    for round_no in range(cut_count):
        coarse_outs = []
        for local_no in range(local_count):
            slice_no = cut_index * local_count + local_no
            coarse_out = stepper(coarse_state, profile_at(slice_no, 0))
            coarse_outs.append(cropper(coarse_out))
            coarse_state = coarse_out + states[2 + 2 * local_no : 4 + 2 * local_no]
        if round_no + 1 < cut_count:
            received = shifted(coarse_state, "cuts", 1)
            coarse_state = jnp.where(cut_index == 0, first_state, received)
    coarse_new = jnp.stack(coarse_outs)
    ends = prolong(coarse_new) + jnp.stack(corrections)
    return (ends, coarse_new)


def solution(mesh):
    placed = (
        P(("grp", "cuts"), None, ("space", "sub"), None),
        P(("grp", "cuts"), None, ("space", "sub"), None),
        P(("grp", "space", "sub"), None),
        P(),
        P("grp"),
        P(),
    )
    return jax.shard_map(
        local,
        mesh=mesh,
        in_specs=placed,
        out_specs=(
            P(("grp", "cuts"), None, ("space", "sub"), None),
            P(("grp", "cuts"), None, ("space", "sub"), None),
        ),
        check_vma=False,
    )
```

profile of v0, /device:TPU:15, one launch (start us, length us, event | category | flops | bytes accessed | tf_op | source)
XLA Modules:
  0.0 173.6 jit_solution(1229046605786915167)
XLA Ops:
  1.4 2.6 %collective-permute-start.1 = (s32[4,512]{1,0:T(4,128)S(1)}, s32[4,512]{1,0:T(4,128)S(1)}, u32[]{:S(2)}, u32[]{:S(2)}) collective-permute-start(s32[4,512]{1,0:T(4,128)S(1)} %get-tuple-element.96), channel_id=1, source_target_pairs={{1,0},{4,1},{5,4},{8,5},{9,8},{12,9},{13,12},{3,2},{6,3},{7,6},{10... | collective-permute-start | bytes 24584 | tf_op jit(solution)/shard_map/ppermute | solution.py:20
  4.0 3.1 %collective-permute-start = (s32[4,512]{1,0:T(4,128)S(1)}, s32[4,512]{1,0:T(4,128)S(1)}, u32[]{:S(2)}, u32[]{:S(2)}) collective-permute-start(s32[4,512]{1,0:T(4,128)S(1)} %get-tuple-element.95), channel_id=1, source_target_pairs={{0,1},{1,4},{4,5},{5,8},{8,9},{9,12},{12,13},{2,3},{3,6},{6,7},{7,... | collective-permute-start | bytes 24584 | tf_op jit(solution)/shard_map/ppermute | solution.py:17
  7.1 1.2 fusion.195
  8.3 5.7 %reshape_squeeze.3 = f32[2,8,4,128,4]{4,3,2,1,0:T(8,128)} reshape(f32[1,2,32,512]{3,2,1,0:T(8,128)S(1)} %get-tuple-element.48) | data formatting | bytes 262144 | tf_op jit(solution)/shard_map/reshape;squeeze | solution.py:33
  14.0 2.5 %reduce_sum.66 = f32[2,8,128]{2,1,0:T(8,128)S(1)} reduce(f32[2,8,4,128,4]{4,3,2,1,0:T(8,128)} %reshape_squeeze.3, f32[]{:T(128)} %constant.120.clone.1), dimensions={2,4}, to_apply=%region_1.2 | reduce | flops 30720 | bytes 139268 | tf_op jit(solution)/shard_map/reduce_sum | solution.py:34
  16.5 1.9 %collective-permute-start.2 = (f32[2,1,128]{2,1,0:T(1,128)S(1)}, f32[2,1,128]{2,1,0:T(1,128)S(1)}, u32[]{:S(2)}, u32[]{:S(2)}) collective-permute-start(f32[2,1,128]{2,1,0:T(1,128)S(1)} %get-tuple-element.122), channel_id=1, source_target_pairs={{1,0},{4,1},{5,4},{8,5},{9,8},{12,9},{13,12},{3,2},{6,3},{7,6},{10... | collective-permute-start | bytes 3080 | tf_op jit(solution)/shard_map/ppermute | solution.py:20
  18.5 3.6 %collective-permute-start.3 = (f32[2,1,128]{2,1,0:T(1,128)S(1)}, f32[2,1,128]{2,1,0:T(1,128)S(1)}, u32[]{:S(2)}, u32[]{:S(2)}) collective-permute-start(f32[2,1,128]{2,1,0:T(1,128)S(1)} %get-tuple-element.121), channel_id=1, source_target_pairs={{0,1},{1,4},{4,5},{5,8},{8,9},{9,12},{12,13},{2,3},{3,6},{6,7},{7,... | collective-permute-start | bytes 3080 | tf_op jit(solution)/shard_map/ppermute | solution.py:17
  22.1 1.9 %collective-permute-start.22 = (f32[2,1,512]{2,1,0:T(1,128)S(1)}, f32[2,1,512]{2,1,0:T(1,128)S(1)}, u32[]{:S(2)}, u32[]{:S(2)}) collective-permute-start(f32[2,1,512]{2,1,0:T(1,128)S(1)} %get-tuple-element.70), channel_id=1, source_target_pairs={{1,0},{4,1},{5,4},{8,5},{9,8},{12,9},{13,12},{3,2},{6,3},{7,6},{10... | collective-permute-start | bytes 12296 | tf_op jit(solution)/shard_map/ppermute | solution.py:20
  41.0 3.6 %collective-permute-start.23 = (f32[2,1,512]{2,1,0:T(1,128)S(1)}, f32[2,1,512]{2,1,0:T(1,128)S(1)}, u32[]{:S(2)}, u32[]{:S(2)}) collective-permute-start(f32[2,1,512]{2,1,0:T(1,128)S(1)} %get-tuple-element.69), channel_id=1, source_target_pairs={{0,1},{1,4},{4,5},{5,8},{8,9},{9,12},{12,13},{2,3},{3,6},{6,7},{7,... | collective-permute-start | bytes 12296 | tf_op jit(solution)/shard_map/ppermute | solution.py:17
  44.7 1.9 %collective-permute-start.4 = (f32[2,1,512]{2,1,0:T(1,128)S(1)}, f32[2,1,512]{2,1,0:T(1,128)S(1)}, u32[]{:S(2)}, u32[]{:S(2)}) collective-permute-start(f32[2,1,512]{2,1,0:T(1,128)S(1)} %get-tuple-element.60), channel_id=1, source_target_pairs={{1,0},{4,1},{5,4},{8,5},{9,8},{12,9},{13,12},{3,2},{6,3},{7,6},{10... | collective-permute-start | bytes 12296 | tf_op jit(solution)/shard_map/ppermute | solution.py:20
  46.7 3.6 %collective-permute-start.5 = (f32[2,1,512]{2,1,0:T(1,128)S(1)}, f32[2,1,512]{2,1,0:T(1,128)S(1)}, u32[]{:S(2)}, u32[]{:S(2)}) collective-permute-start(f32[2,1,512]{2,1,0:T(1,128)S(1)} %get-tuple-element.59), channel_id=1, source_target_pairs={{0,1},{1,4},{4,5},{5,8},{8,9},{9,12},{12,13},{2,3},{3,6},{6,7},{7,... | collective-permute-start | bytes 12296 | tf_op jit(solution)/shard_map/ppermute | solution.py:17
  50.4 1.9 %collective-permute-start.16 = (f32[2,1,512]{2,1,0:T(1,128)S(1)}, f32[2,1,512]{2,1,0:T(1,128)S(1)}, u32[]{:S(2)}, u32[]{:S(2)}) collective-permute-start(f32[2,1,512]{2,1,0:T(1,128)S(1)} %get-tuple-element.68), channel_id=1, source_target_pairs={{1,0},{4,1},{5,4},{8,5},{9,8},{12,9},{13,12},{3,2},{6,3},{7,6},{10... | collective-permute-start | bytes 12296 | tf_op jit(solution)/shard_map/ppermute | solution.py:20
  52.4 3.6 %collective-permute-start.17 = (f32[2,1,512]{2,1,0:T(1,128)S(1)}, f32[2,1,512]{2,1,0:T(1,128)S(1)}, u32[]{:S(2)}, u32[]{:S(2)}) collective-permute-start(f32[2,1,512]{2,1,0:T(1,128)S(1)} %get-tuple-element.67), channel_id=1, source_target_pairs={{0,1},{1,4},{4,5},{5,8},{8,9},{9,12},{12,13},{2,3},{3,6},{6,7},{7,... | collective-permute-start | bytes 12296 | tf_op jit(solution)/shard_map/ppermute | solution.py:17
  56.1 1.9 %collective-permute-start.10 = (f32[2,1,512]{2,1,0:T(1,128)S(1)}, f32[2,1,512]{2,1,0:T(1,128)S(1)}, u32[]{:S(2)}, u32[]{:S(2)}) collective-permute-start(f32[2,1,512]{2,1,0:T(1,128)S(1)} %get-tuple-element.64), channel_id=1, source_target_pairs={{1,0},{4,1},{5,4},{8,5},{9,8},{12,9},{13,12},{3,2},{6,3},{7,6},{10... | collective-permute-start | bytes 12296 | tf_op jit(solution)/shard_map/ppermute | solution.py:20
  58.2 3.8 %collective-permute-start.11 = (f32[2,1,512]{2,1,0:T(1,128)S(1)}, f32[2,1,512]{2,1,0:T(1,128)S(1)}, u32[]{:S(2)}, u32[]{:S(2)}) collective-permute-start(f32[2,1,512]{2,1,0:T(1,128)S(1)} %get-tuple-element.63), channel_id=1, source_target_pairs={{0,1},{1,4},{4,5},{5,8},{8,9},{9,12},{12,13},{2,3},{3,6},{6,7},{7,... | collective-permute-start | bytes 12296 | tf_op jit(solution)/shard_map/ppermute | solution.py:17
  64.0 1.6 copy.471
  65.6 1.0 broadcast_in_dim.217
  66.6 1.6 copy.470
  69.2 1.6 copy.469
  71.8 1.6 copy.468
  74.4 1.6 copy.467
  77.1 1.8 %copy.466 = pred[10,4,130,4]{2,3,1,0:T(4,128)(4,1)S(1)} copy(pred[10,4,130,4]{3,2,1,0:T(8,128)(4,1)S(1)} %broadcast_in_dim.201) | data formatting | bytes 41600 | tf_op jit(solution)/shard_map/jit(_where)/broadcast_in_dim | solution.py:45
  79.9 1.6 copy.465
  82.5 1.6 copy.464
  86.5 3.0 %collective-permute-start.6 = (f32[2,1,512]{2,1,0:T(1,128)S(1)}, f32[2,1,512]{2,1,0:T(1,128)S(1)}, u32[]{:S(2)}, u32[]{:S(2)}) collective-permute-start(f32[2,1,512]{2,1,0:T(1,128)S(1)} %get-tuple-element.58), channel_id=1, source_target_pairs={{1,0},{4,1},{5,4},{8,5},{9,8},{12,9},{13,12},{3,2},{6,3},{7,6},{10... | collective-permute-start | bytes 12296 | tf_op jit(solution)/shard_map/ppermute | solution.py:20
  89.5 3.1 %collective-permute-start.7 = (f32[2,1,512]{2,1,0:T(1,128)S(1)}, f32[2,1,512]{2,1,0:T(1,128)S(1)}, u32[]{:S(2)}, u32[]{:S(2)}) collective-permute-start(f32[2,1,512]{2,1,0:T(1,128)S(1)} %get-tuple-element.57), channel_id=1, source_target_pairs={{0,1},{1,4},{4,5},{5,8},{8,9},{9,12},{12,13},{2,3},{3,6},{6,7},{7,... | collective-permute-start | bytes 12296 | tf_op jit(solution)/shard_map/ppermute | solution.py:17
  93.4 1.9 %collective-permute-start.12 = (f32[2,1,512]{2,1,0:T(1,128)S(1)}, f32[2,1,512]{2,1,0:T(1,128)S(1)}, u32[]{:S(2)}, u32[]{:S(2)}) collective-permute-start(f32[2,1,512]{2,1,0:T(1,128)S(1)} %get-tuple-element.62), channel_id=1, source_target_pairs={{1,0},{4,1},{5,4},{8,5},{9,8},{12,9},{13,12},{3,2},{6,3},{7,6},{10... | collective-permute-start | bytes 12296 | tf_op jit(solution)/shard_map/ppermute | solution.py:20
  95.4 3.6 %collective-permute-start.13 = (f32[2,1,512]{2,1,0:T(1,128)S(1)}, f32[2,1,512]{2,1,0:T(1,128)S(1)}, u32[]{:S(2)}, u32[]{:S(2)}) collective-permute-start(f32[2,1,512]{2,1,0:T(1,128)S(1)} %get-tuple-element.61), channel_id=1, source_target_pairs={{0,1},{1,4},{4,5},{5,8},{8,9},{9,12},{12,13},{2,3},{3,6},{6,7},{7,... | collective-permute-start | bytes 12296 | tf_op jit(solution)/shard_map/ppermute | solution.py:17
  99.8 1.9 %collective-permute-start.18 = (f32[2,1,512]{2,1,0:T(1,128)S(1)}, f32[2,1,512]{2,1,0:T(1,128)S(1)}, u32[]{:S(2)}, u32[]{:S(2)}) collective-permute-start(f32[2,1,512]{2,1,0:T(1,128)S(1)} %get-tuple-element.66), channel_id=1, source_target_pairs={{1,0},{4,1},{5,4},{8,5},{9,8},{12,9},{13,12},{3,2},{6,3},{7,6},{10... | collective-permute-start | bytes 12296 | tf_op jit(solution)/shard_map/ppermute | solution.py:20
  102.7 3.6 %collective-permute-start.19 = (f32[2,1,512]{2,1,0:T(1,128)S(1)}, f32[2,1,512]{2,1,0:T(1,128)S(1)}, u32[]{:S(2)}, u32[]{:S(2)}) collective-permute-start(f32[2,1,512]{2,1,0:T(1,128)S(1)} %get-tuple-element.65), channel_id=1, source_target_pairs={{0,1},{1,4},{4,5},{5,8},{8,9},{9,12},{12,13},{2,3},{3,6},{6,7},{7,... | collective-permute-start | bytes 12296 | tf_op jit(solution)/shard_map/ppermute | solution.py:17
  106.4 1.9 %collective-permute-start.24 = (f32[2,1,512]{2,1,0:T(1,128)S(1)}, f32[2,1,512]{2,1,0:T(1,128)S(1)}, u32[]{:S(2)}, u32[]{:S(2)}) collective-permute-start(f32[2,1,512]{2,1,0:T(1,128)S(1)} %get-tuple-element.56), channel_id=1, source_target_pairs={{1,0},{4,1},{5,4},{8,5},{9,8},{12,9},{13,12},{3,2},{6,3},{7,6},{10... | collective-permute-start | bytes 12296 | tf_op jit(solution)/shard_map/ppermute | solution.py:20
  110.0 3.6 %collective-permute-start.25 = (f32[2,1,512]{2,1,0:T(1,128)S(1)}, f32[2,1,512]{2,1,0:T(1,128)S(1)}, u32[]{:S(2)}, u32[]{:S(2)}) collective-permute-start(f32[2,1,512]{2,1,0:T(1,128)S(1)} %get-tuple-element.55), channel_id=1, source_target_pairs={{0,1},{1,4},{4,5},{5,8},{8,9},{9,12},{12,13},{2,3},{3,6},{6,7},{7,... | collective-permute-start | bytes 12296 | tf_op jit(solution)/shard_map/ppermute | solution.py:17
  113.6 1.9 %collective-permute-start.8 = (f32[2,1,128]{2,1,0:T(1,128)S(1)}, f32[2,1,128]{2,1,0:T(1,128)S(1)}, u32[]{:S(2)}, u32[]{:S(2)}) collective-permute-start(f32[2,1,128]{2,1,0:T(1,128)S(1)} %get-tuple-element.120), channel_id=1, source_target_pairs={{1,0},{4,1},{5,4},{8,5},{9,8},{12,9},{13,12},{3,2},{6,3},{7,6},{10... | collective-permute-start | bytes 3080 | tf_op jit(solution)/shard_map/ppermute | solution.py:20
  116.6 3.6 %collective-permute-start.9 = (f32[2,1,128]{2,1,0:T(1,128)S(1)}, f32[2,1,128]{2,1,0:T(1,128)S(1)}, u32[]{:S(2)}, u32[]{:S(2)}) collective-permute-start(f32[2,1,128]{2,1,0:T(1,128)S(1)} %get-tuple-element.119), channel_id=1, source_target_pairs={{0,1},{1,4},{4,5},{5,8},{8,9},{9,12},{12,13},{2,3},{3,6},{6,7},{7,... | collective-permute-start | bytes 3080 | tf_op jit(solution)/shard_map/ppermute | solution.py:17
  123.7 1.9 %collective-permute-start.14 = (f32[2,1,128]{2,1,0:T(1,128)S(1)}, f32[2,1,128]{2,1,0:T(1,128)S(1)}, u32[]{:S(2)}, u32[]{:S(2)}) collective-permute-start(f32[2,1,128]{2,1,0:T(1,128)S(1)} %get-tuple-element.118), channel_id=1, source_target_pairs={{1,0},{4,1},{5,4},{8,5},{9,8},{12,9},{13,12},{3,2},{6,3},{7,6},{10... | collective-permute-start | bytes 3080 | tf_op jit(solution)/shard_map/ppermute | solution.py:20
  125.6 3.6 %collective-permute-start.15 = (f32[2,1,128]{2,1,0:T(1,128)S(1)}, f32[2,1,128]{2,1,0:T(1,128)S(1)}, u32[]{:S(2)}, u32[]{:S(2)}) collective-permute-start(f32[2,1,128]{2,1,0:T(1,128)S(1)} %get-tuple-element.117), channel_id=1, source_target_pairs={{0,1},{1,4},{4,5},{5,8},{8,9},{9,12},{12,13},{2,3},{3,6},{6,7},{7,... | collective-permute-start | bytes 3080 | tf_op jit(solution)/shard_map/ppermute | solution.py:17
  130.2 3.0 %collective-permute-start.20 = (f32[2,1,128]{2,1,0:T(1,128)S(1)}, f32[2,1,128]{2,1,0:T(1,128)S(1)}, u32[]{:S(2)}, u32[]{:S(2)}) collective-permute-start(f32[2,1,128]{2,1,0:T(1,128)S(1)} %get-tuple-element.116), channel_id=1, source_target_pairs={{1,0},{4,1},{5,4},{8,5},{9,8},{12,9},{13,12},{3,2},{6,3},{7,6},{10... | collective-permute-start | bytes 3080 | tf_op jit(solution)/shard_map/ppermute | solution.py:20
  133.2 3.1 %collective-permute-start.21 = (f32[2,1,128]{2,1,0:T(1,128)S(1)}, f32[2,1,128]{2,1,0:T(1,128)S(1)}, u32[]{:S(2)}, u32[]{:S(2)}) collective-permute-start(f32[2,1,128]{2,1,0:T(1,128)S(1)} %get-tuple-element.115), channel_id=1, source_target_pairs={{0,1},{1,4},{4,5},{5,8},{8,9},{9,12},{12,13},{2,3},{3,6},{6,7},{7,... | collective-permute-start | bytes 3080 | tf_op jit(solution)/shard_map/ppermute | solution.py:17
  137.3 1.3 collective-permute-start.26
  138.6 3.1 %collective-permute-done.26 = f32[2,8,128]{2,1,0:T(8,128)S(1)} collective-permute-done((f32[2,8,128]{2,1,0:T(8,128)S(1)}, f32[2,8,128]{2,1,0:T(8,128)S(1)}, u32[]{:S(2)}, u32[]{:S(2)}) %collective-permute-start.26) | collective-permute-done | bytes 8224 | tf_op jit(solution)/shard_map/ppermute | solution.py:28
  141.7 4.1 %collective-permute-start.27 = (f32[2,1,128]{2,1,0:T(1,128)S(1)}, f32[2,1,128]{2,1,0:T(1,128)S(1)}, u32[]{:S(2)}, u32[]{:S(2)}) collective-permute-start(f32[2,1,128]{2,1,0:T(1,128)S(1)} %get-tuple-element.114), channel_id=1, source_target_pairs={{1,0},{4,1},{5,4},{8,5},{9,8},{12,9},{13,12},{3,2},{6,3},{7,6},{10... | collective-permute-start | bytes 3080 | tf_op jit(solution)/shard_map/ppermute | solution.py:20
  145.8 3.1 %collective-permute-start.28 = (f32[2,1,128]{2,1,0:T(1,128)S(1)}, f32[2,1,128]{2,1,0:T(1,128)S(1)}, u32[]{:S(2)}, u32[]{:S(2)}) collective-permute-start(f32[2,1,128]{2,1,0:T(1,128)S(1)} %get-tuple-element.113), channel_id=1, source_target_pairs={{0,1},{1,4},{4,5},{5,8},{8,9},{9,12},{12,13},{2,3},{3,6},{6,7},{7,... | collective-permute-start | bytes 3080 | tf_op jit(solution)/shard_map/ppermute | solution.py:17
  149.9 3.0 %collective-permute-start.29 = (f32[2,1,128]{2,1,0:T(1,128)S(1)}, f32[2,1,128]{2,1,0:T(1,128)S(1)}, u32[]{:S(2)}, u32[]{:S(2)}) collective-permute-start(f32[2,1,128]{2,1,0:T(1,128)S(1)} %get-tuple-element.112), channel_id=1, source_target_pairs={{1,0},{4,1},{5,4},{8,5},{9,8},{12,9},{13,12},{3,2},{6,3},{7,6},{10... | collective-permute-start | bytes 3080 | tf_op jit(solution)/shard_map/ppermute | solution.py:20
  152.9 3.1 %collective-permute-start.30 = (f32[2,1,128]{2,1,0:T(1,128)S(1)}, f32[2,1,128]{2,1,0:T(1,128)S(1)}, u32[]{:S(2)}, u32[]{:S(2)}) collective-permute-start(f32[2,1,128]{2,1,0:T(1,128)S(1)} %get-tuple-element.111), channel_id=1, source_target_pairs={{0,1},{1,4},{4,5},{5,8},{8,9},{9,12},{12,13},{2,3},{3,6},{6,7},{7,... | collective-permute-start | bytes 3080 | tf_op jit(solution)/shard_map/ppermute | solution.py:17
  157.8 2.2 %collective-permute-start.31 = (f32[2,1,128]{2,1,0:T(1,128)S(1)}, f32[2,1,128]{2,1,0:T(1,128)S(1)}, u32[]{:S(2)}, u32[]{:S(2)}) collective-permute-start(f32[2,1,128]{2,1,0:T(1,128)S(1)} %get-tuple-element.110), channel_id=1, source_target_pairs={{1,0},{4,1},{5,4},{8,5},{9,8},{12,9},{13,12},{3,2},{6,3},{7,6},{10... | collective-permute-start | bytes 3080 | tf_op jit(solution)/shard_map/ppermute | solution.py:20
  160.0 3.4 %collective-permute-start.32 = (f32[2,1,128]{2,1,0:T(1,128)S(1)}, f32[2,1,128]{2,1,0:T(1,128)S(1)}, u32[]{:S(2)}, u32[]{:S(2)}) collective-permute-start(f32[2,1,128]{2,1,0:T(1,128)S(1)} %get-tuple-element.109), channel_id=1, source_target_pairs={{0,1},{1,4},{4,5},{5,8},{8,9},{9,12},{12,13},{2,3},{3,6},{6,7},{7,... | collective-permute-start | bytes 3080 | tf_op jit(solution)/shard_map/ppermute | solution.py:17
  164.4 3.0 %collective-permute-start.33 = (f32[2,1,128]{2,1,0:T(1,128)S(1)}, f32[2,1,128]{2,1,0:T(1,128)S(1)}, u32[]{:S(2)}, u32[]{:S(2)}) collective-permute-start(f32[2,1,128]{2,1,0:T(1,128)S(1)} %get-tuple-element.108), channel_id=1, source_target_pairs={{1,0},{4,1},{5,4},{8,5},{9,8},{12,9},{13,12},{3,2},{6,3},{7,6},{10... | collective-permute-start | bytes 3080 | tf_op jit(solution)/shard_map/ppermute | solution.py:20
  167.4 3.1 %collective-permute-start.34 = (f32[2,1,128]{2,1,0:T(1,128)S(1)}, f32[2,1,128]{2,1,0:T(1,128)S(1)}, u32[]{:S(2)}, u32[]{:S(2)}) collective-permute-start(f32[2,1,128]{2,1,0:T(1,128)S(1)} %get-tuple-element.107), channel_id=1, source_target_pairs={{0,1},{1,4},{4,5},{5,8},{8,9},{9,12},{12,13},{2,3},{3,6},{6,7},{7,... | collective-permute-start | bytes 3080 | tf_op jit(solution)/shard_map/ppermute | solution.py:17
  (188 shorter events, 29.9 us)
Async XLA Ops:
  1.4 61.3 %collective-permute-start.1 = (s32[4,512]{1,0:T(4,128)S(1)}, s32[4,512]{1,0:T(4,128)S(1)}, u32[]{:S(2)}, u32[]{:S(2)}) collective-permute-start(s32[4,512]{1,0:T(4,128)S(1)} %get-tuple-element.96), channel_id=1, source_target_pairs={{1,0},{4,1},{5,4},{8,5},{9,8},{12,9},{13,12},{3,2},{6,3},{7,6},{10... | collective-permute-start | bytes 24584 | tf_op jit(solution)/shard_map/ppermute | solution.py:20
  4.0 58.8 %collective-permute-start = (s32[4,512]{1,0:T(4,128)S(1)}, s32[4,512]{1,0:T(4,128)S(1)}, u32[]{:S(2)}, u32[]{:S(2)}) collective-permute-start(s32[4,512]{1,0:T(4,128)S(1)} %get-tuple-element.95), channel_id=1, source_target_pairs={{0,1},{1,4},{4,5},{5,8},{8,9},{9,12},{12,13},{2,3},{3,6},{6,7},{7,... | collective-permute-start | bytes 24584 | tf_op jit(solution)/shard_map/ppermute | solution.py:17
  8.2 15.8 %copy-start.5 = (s32[8]{0:T(128)S(1)}, s32[8]{0:T(128)}, u32[]{:S(2)}) copy-start(s32[8]{0:T(128)} %param.11) | copy-start | bytes 100
  8.2 26.6 %copy-start.2 = (f32[4,8]{1,0:T(4,128)S(1)}, f32[4,8]{1,0:T(4,128)}, u32[]{:S(2)}) copy-start(f32[4,8]{1,0:T(4,128)} %param.9) | copy-start | bytes 388
  8.3 26.9 %copy-start.6 = (s32[96]{0:T(128)S(1)}, s32[96]{0:T(128)}, u32[]{:S(2)}) copy-start(s32[96]{0:T(128)} %param.10) | copy-start | bytes 1156
  8.3 26.9 %copy-start.4 = (f32[4,2,8,128]{3,2,1,0:T(8,128)S(1)}, f32[4,2,8,128]{3,2,1,0:T(8,128)}, u32[]{:S(2)}) copy-start(f32[4,2,8,128]{3,2,1,0:T(8,128)} %param.7) | copy-start | bytes 98308
  8.3 54.5 %copy-start.3 = (s32[32,512]{1,0:T(8,128)S(1)}, s32[32,512]{1,0:T(8,128)}, u32[]{:S(2)}) copy-start(s32[32,512]{1,0:T(8,128)} %param.8) | copy-start | bytes 196612
  16.5 24.5 %collective-permute-start.2 = (f32[2,1,128]{2,1,0:T(1,128)S(1)}, f32[2,1,128]{2,1,0:T(1,128)S(1)}, u32[]{:S(2)}, u32[]{:S(2)}) collective-permute-start(f32[2,1,128]{2,1,0:T(1,128)S(1)} %get-tuple-element.122), channel_id=1, source_target_pairs={{1,0},{4,1},{5,4},{8,5},{9,8},{12,9},{13,12},{3,2},{6,3},{7,6},{10... | collective-permute-start | bytes 3080 | tf_op jit(solution)/shard_map/ppermute | solution.py:20
  18.5 26.2 %collective-permute-start.3 = (f32[2,1,128]{2,1,0:T(1,128)S(1)}, f32[2,1,128]{2,1,0:T(1,128)S(1)}, u32[]{:S(2)}, u32[]{:S(2)}) collective-permute-start(f32[2,1,128]{2,1,0:T(1,128)S(1)} %get-tuple-element.121), channel_id=1, source_target_pairs={{0,1},{1,4},{4,5},{5,8},{8,9},{9,12},{12,13},{2,3},{3,6},{6,7},{7,... | collective-permute-start | bytes 3080 | tf_op jit(solution)/shard_map/ppermute | solution.py:17
  22.1 24.6 %collective-permute-start.22 = (f32[2,1,512]{2,1,0:T(1,128)S(1)}, f32[2,1,512]{2,1,0:T(1,128)S(1)}, u32[]{:S(2)}, u32[]{:S(2)}) collective-permute-start(f32[2,1,512]{2,1,0:T(1,128)S(1)} %get-tuple-element.70), channel_id=1, source_target_pairs={{1,0},{4,1},{5,4},{8,5},{9,8},{12,9},{13,12},{3,2},{6,3},{7,6},{10... | collective-permute-start | bytes 12296 | tf_op jit(solution)/shard_map/ppermute | solution.py:20
  41.0 9.3 %collective-permute-start.23 = (f32[2,1,512]{2,1,0:T(1,128)S(1)}, f32[2,1,512]{2,1,0:T(1,128)S(1)}, u32[]{:S(2)}, u32[]{:S(2)}) collective-permute-start(f32[2,1,512]{2,1,0:T(1,128)S(1)} %get-tuple-element.69), channel_id=1, source_target_pairs={{0,1},{1,4},{4,5},{5,8},{8,9},{9,12},{12,13},{2,3},{3,6},{6,7},{7,... | collective-permute-start | bytes 12296 | tf_op jit(solution)/shard_map/ppermute | solution.py:17
  44.7 7.8 %collective-permute-start.4 = (f32[2,1,512]{2,1,0:T(1,128)S(1)}, f32[2,1,512]{2,1,0:T(1,128)S(1)}, u32[]{:S(2)}, u32[]{:S(2)}) collective-permute-start(f32[2,1,512]{2,1,0:T(1,128)S(1)} %get-tuple-element.60), channel_id=1, source_target_pairs={{1,0},{4,1},{5,4},{8,5},{9,8},{12,9},{13,12},{3,2},{6,3},{7,6},{10... | collective-permute-start | bytes 12296 | tf_op jit(solution)/shard_map/ppermute | solution.py:20
  46.7 9.4 %collective-permute-start.5 = (f32[2,1,512]{2,1,0:T(1,128)S(1)}, f32[2,1,512]{2,1,0:T(1,128)S(1)}, u32[]{:S(2)}, u32[]{:S(2)}) collective-permute-start(f32[2,1,512]{2,1,0:T(1,128)S(1)} %get-tuple-element.59), channel_id=1, source_target_pairs={{0,1},{1,4},{4,5},{5,8},{8,9},{9,12},{12,13},{2,3},{3,6},{6,7},{7,... | collective-permute-start | bytes 12296 | tf_op jit(solution)/shard_map/ppermute | solution.py:17
  50.4 7.8 %collective-permute-start.16 = (f32[2,1,512]{2,1,0:T(1,128)S(1)}, f32[2,1,512]{2,1,0:T(1,128)S(1)}, u32[]{:S(2)}, u32[]{:S(2)}) collective-permute-start(f32[2,1,512]{2,1,0:T(1,128)S(1)} %get-tuple-element.68), channel_id=1, source_target_pairs={{1,0},{4,1},{5,4},{8,5},{9,8},{12,9},{13,12},{3,2},{6,3},{7,6},{10... | collective-permute-start | bytes 12296 | tf_op jit(solution)/shard_map/ppermute | solution.py:20
  52.4 9.6 %collective-permute-start.17 = (f32[2,1,512]{2,1,0:T(1,128)S(1)}, f32[2,1,512]{2,1,0:T(1,128)S(1)}, u32[]{:S(2)}, u32[]{:S(2)}) collective-permute-start(f32[2,1,512]{2,1,0:T(1,128)S(1)} %get-tuple-element.67), channel_id=1, source_target_pairs={{0,1},{1,4},{4,5},{5,8},{8,9},{9,12},{12,13},{2,3},{3,6},{6,7},{7,... | collective-permute-start | bytes 12296 | tf_op jit(solution)/shard_map/ppermute | solution.py:17
  56.1 6.1 %collective-permute-start.10 = (f32[2,1,512]{2,1,0:T(1,128)S(1)}, f32[2,1,512]{2,1,0:T(1,128)S(1)}, u32[]{:S(2)}, u32[]{:S(2)}) collective-permute-start(f32[2,1,512]{2,1,0:T(1,128)S(1)} %get-tuple-element.64), channel_id=1, source_target_pairs={{1,0},{4,1},{5,4},{8,5},{9,8},{12,9},{13,12},{3,2},{6,3},{7,6},{10... | collective-permute-start | bytes 12296 | tf_op jit(solution)/shard_map/ppermute | solution.py:20
  58.2 4.4 %collective-permute-start.11 = (f32[2,1,512]{2,1,0:T(1,128)S(1)}, f32[2,1,512]{2,1,0:T(1,128)S(1)}, u32[]{:S(2)}, u32[]{:S(2)}) collective-permute-start(f32[2,1,512]{2,1,0:T(1,128)S(1)} %get-tuple-element.63), channel_id=1, source_target_pairs={{0,1},{1,4},{4,5},{5,8},{8,9},{9,12},{12,13},{2,3},{3,6},{6,7},{7,... | collective-permute-start | bytes 12296 | tf_op jit(solution)/shard_map/ppermute | solution.py:17
  77.1 8.6 %copy-start = (f32[4,2,32,512]{3,2,1,0:T(8,128)S(1)}, f32[4,2,32,512]{3,2,1,0:T(8,128)}, u32[]{:S(2)}) copy-start(f32[4,2,32,512]{3,2,1,0:T(8,128)} %param.6) | copy-start | bytes 1572868
  86.5 16.3 %collective-permute-start.6 = (f32[2,1,512]{2,1,0:T(1,128)S(1)}, f32[2,1,512]{2,1,0:T(1,128)S(1)}, u32[]{:S(2)}, u32[]{:S(2)}) collective-permute-start(f32[2,1,512]{2,1,0:T(1,128)S(1)} %get-tuple-element.58), channel_id=1, source_target_pairs={{1,0},{4,1},{5,4},{8,5},{9,8},{12,9},{13,12},{3,2},{6,3},{7,6},{10... | collective-permute-start | bytes 12296 | tf_op jit(solution)/shard_map/ppermute | solution.py:20
  89.5 16.9 %collective-permute-start.7 = (f32[2,1,512]{2,1,0:T(1,128)S(1)}, f32[2,1,512]{2,1,0:T(1,128)S(1)}, u32[]{:S(2)}, u32[]{:S(2)}) collective-permute-start(f32[2,1,512]{2,1,0:T(1,128)S(1)} %get-tuple-element.57), channel_id=1, source_target_pairs={{0,1},{1,4},{4,5},{5,8},{8,9},{9,12},{12,13},{2,3},{3,6},{6,7},{7,... | collective-permute-start | bytes 12296 | tf_op jit(solution)/shard_map/ppermute | solution.py:17
  93.4 16.5 %collective-permute-start.12 = (f32[2,1,512]{2,1,0:T(1,128)S(1)}, f32[2,1,512]{2,1,0:T(1,128)S(1)}, u32[]{:S(2)}, u32[]{:S(2)}) collective-permute-start(f32[2,1,512]{2,1,0:T(1,128)S(1)} %get-tuple-element.62), channel_id=1, source_target_pairs={{1,0},{4,1},{5,4},{8,5},{9,8},{12,9},{13,12},{3,2},{6,3},{7,6},{10... | collective-permute-start | bytes 12296 | tf_op jit(solution)/shard_map/ppermute | solution.py:20
  95.4 18.2 %collective-permute-start.13 = (f32[2,1,512]{2,1,0:T(1,128)S(1)}, f32[2,1,512]{2,1,0:T(1,128)S(1)}, u32[]{:S(2)}, u32[]{:S(2)}) collective-permute-start(f32[2,1,512]{2,1,0:T(1,128)S(1)} %get-tuple-element.61), channel_id=1, source_target_pairs={{0,1},{1,4},{4,5},{5,8},{8,9},{9,12},{12,13},{2,3},{3,6},{6,7},{7,... | collective-permute-start | bytes 12296 | tf_op jit(solution)/shard_map/ppermute | solution.py:17
  99.8 16.8 %collective-permute-start.18 = (f32[2,1,512]{2,1,0:T(1,128)S(1)}, f32[2,1,512]{2,1,0:T(1,128)S(1)}, u32[]{:S(2)}, u32[]{:S(2)}) collective-permute-start(f32[2,1,512]{2,1,0:T(1,128)S(1)} %get-tuple-element.66), channel_id=1, source_target_pairs={{1,0},{4,1},{5,4},{8,5},{9,8},{12,9},{13,12},{3,2},{6,3},{7,6},{10... | collective-permute-start | bytes 12296 | tf_op jit(solution)/shard_map/ppermute | solution.py:20
  102.7 17.5 %collective-permute-start.19 = (f32[2,1,512]{2,1,0:T(1,128)S(1)}, f32[2,1,512]{2,1,0:T(1,128)S(1)}, u32[]{:S(2)}, u32[]{:S(2)}) collective-permute-start(f32[2,1,512]{2,1,0:T(1,128)S(1)} %get-tuple-element.65), channel_id=1, source_target_pairs={{0,1},{1,4},{4,5},{5,8},{8,9},{9,12},{12,13},{2,3},{3,6},{6,7},{7,... | collective-permute-start | bytes 12296 | tf_op jit(solution)/shard_map/ppermute | solution.py:17
  106.4 15.3 %collective-permute-start.24 = (f32[2,1,512]{2,1,0:T(1,128)S(1)}, f32[2,1,512]{2,1,0:T(1,128)S(1)}, u32[]{:S(2)}, u32[]{:S(2)}) collective-permute-start(f32[2,1,512]{2,1,0:T(1,128)S(1)} %get-tuple-element.56), channel_id=1, source_target_pairs={{1,0},{4,1},{5,4},{8,5},{9,8},{12,9},{13,12},{3,2},{6,3},{7,6},{10... | collective-permute-start | bytes 12296 | tf_op jit(solution)/shard_map/ppermute | solution.py:20
  110.0 11.8 %collective-permute-start.25 = (f32[2,1,512]{2,1,0:T(1,128)S(1)}, f32[2,1,512]{2,1,0:T(1,128)S(1)}, u32[]{:S(2)}, u32[]{:S(2)}) collective-permute-start(f32[2,1,512]{2,1,0:T(1,128)S(1)} %get-tuple-element.55), channel_id=1, source_target_pairs={{0,1},{1,4},{4,5},{5,8},{8,9},{9,12},{12,13},{2,3},{3,6},{6,7},{7,... | collective-permute-start | bytes 12296 | tf_op jit(solution)/shard_map/ppermute | solution.py:17
  113.6 9.8 %collective-permute-start.8 = (f32[2,1,128]{2,1,0:T(1,128)S(1)}, f32[2,1,128]{2,1,0:T(1,128)S(1)}, u32[]{:S(2)}, u32[]{:S(2)}) collective-permute-start(f32[2,1,128]{2,1,0:T(1,128)S(1)} %get-tuple-element.120), channel_id=1, source_target_pairs={{1,0},{4,1},{5,4},{8,5},{9,8},{12,9},{13,12},{3,2},{6,3},{7,6},{10... | collective-permute-start | bytes 3080 | tf_op jit(solution)/shard_map/ppermute | solution.py:20
  116.6 6.8 %collective-permute-start.9 = (f32[2,1,128]{2,1,0:T(1,128)S(1)}, f32[2,1,128]{2,1,0:T(1,128)S(1)}, u32[]{:S(2)}, u32[]{:S(2)}) collective-permute-start(f32[2,1,128]{2,1,0:T(1,128)S(1)} %get-tuple-element.119), channel_id=1, source_target_pairs={{0,1},{1,4},{4,5},{5,8},{8,9},{9,12},{12,13},{2,3},{3,6},{6,7},{7,... | collective-permute-start | bytes 3080 | tf_op jit(solution)/shard_map/ppermute | solution.py:17
  123.7 6.1 %collective-permute-start.14 = (f32[2,1,128]{2,1,0:T(1,128)S(1)}, f32[2,1,128]{2,1,0:T(1,128)S(1)}, u32[]{:S(2)}, u32[]{:S(2)}) collective-permute-start(f32[2,1,128]{2,1,0:T(1,128)S(1)} %get-tuple-element.118), channel_id=1, source_target_pairs={{1,0},{4,1},{5,4},{8,5},{9,8},{12,9},{13,12},{3,2},{6,3},{7,6},{10... | collective-permute-start | bytes 3080 | tf_op jit(solution)/shard_map/ppermute | solution.py:20
  125.6 4.4 %collective-permute-start.15 = (f32[2,1,128]{2,1,0:T(1,128)S(1)}, f32[2,1,128]{2,1,0:T(1,128)S(1)}, u32[]{:S(2)}, u32[]{:S(2)}) collective-permute-start(f32[2,1,128]{2,1,0:T(1,128)S(1)} %get-tuple-element.117), channel_id=1, source_target_pairs={{0,1},{1,4},{4,5},{5,8},{8,9},{9,12},{12,13},{2,3},{3,6},{6,7},{7,... | collective-permute-start | bytes 3080 | tf_op jit(solution)/shard_map/ppermute | solution.py:17
  130.2 6.2 %collective-permute-start.20 = (f32[2,1,128]{2,1,0:T(1,128)S(1)}, f32[2,1,128]{2,1,0:T(1,128)S(1)}, u32[]{:S(2)}, u32[]{:S(2)}) collective-permute-start(f32[2,1,128]{2,1,0:T(1,128)S(1)} %get-tuple-element.116), channel_id=1, source_target_pairs={{1,0},{4,1},{5,4},{8,5},{9,8},{12,9},{13,12},{3,2},{6,3},{7,6},{10... | collective-permute-start | bytes 3080 | tf_op jit(solution)/shard_map/ppermute | solution.py:20
  133.2 3.8 %collective-permute-start.21 = (f32[2,1,128]{2,1,0:T(1,128)S(1)}, f32[2,1,128]{2,1,0:T(1,128)S(1)}, u32[]{:S(2)}, u32[]{:S(2)}) collective-permute-start(f32[2,1,128]{2,1,0:T(1,128)S(1)} %get-tuple-element.115), channel_id=1, source_target_pairs={{0,1},{1,4},{4,5},{5,8},{8,9},{9,12},{12,13},{2,3},{3,6},{6,7},{7,... | collective-permute-start | bytes 3080 | tf_op jit(solution)/shard_map/ppermute | solution.py:17
  137.3 4.4 %collective-permute-start.26 = (f32[2,8,128]{2,1,0:T(8,128)S(1)}, f32[2,8,128]{2,1,0:T(8,128)S(1)}, u32[]{:S(2)}, u32[]{:S(2)}) collective-permute-start(f32[2,8,128]{2,1,0:T(8,128)S(1)} %maximum_add_fusion.4), channel_id=1, source_target_pairs={{0,2},{1,3},{4,6},{5,7},{8,10},{9,11},{12,14},{13,15},{16,18},{17,... | collective-permute-start | bytes 24584 | tf_op jit(solution)/shard_map/ppermute | solution.py:28
  141.7 7.3 %collective-permute-start.27 = (f32[2,1,128]{2,1,0:T(1,128)S(1)}, f32[2,1,128]{2,1,0:T(1,128)S(1)}, u32[]{:S(2)}, u32[]{:S(2)}) collective-permute-start(f32[2,1,128]{2,1,0:T(1,128)S(1)} %get-tuple-element.114), channel_id=1, source_target_pairs={{1,0},{4,1},{5,4},{8,5},{9,8},{12,9},{13,12},{3,2},{6,3},{7,6},{10... | collective-permute-start | bytes 3080 | tf_op jit(solution)/shard_map/ppermute | solution.py:20
  145.8 3.8 %collective-permute-start.28 = (f32[2,1,128]{2,1,0:T(1,128)S(1)}, f32[2,1,128]{2,1,0:T(1,128)S(1)}, u32[]{:S(2)}, u32[]{:S(2)}) collective-permute-start(f32[2,1,128]{2,1,0:T(1,128)S(1)} %get-tuple-element.113), channel_id=1, source_target_pairs={{0,1},{1,4},{4,5},{5,8},{8,9},{9,12},{12,13},{2,3},{3,6},{6,7},{7,... | collective-permute-start | bytes 3080 | tf_op jit(solution)/shard_map/ppermute | solution.py:17
  149.9 7.6 %collective-permute-start.29 = (f32[2,1,128]{2,1,0:T(1,128)S(1)}, f32[2,1,128]{2,1,0:T(1,128)S(1)}, u32[]{:S(2)}, u32[]{:S(2)}) collective-permute-start(f32[2,1,128]{2,1,0:T(1,128)S(1)} %get-tuple-element.112), channel_id=1, source_target_pairs={{1,0},{4,1},{5,4},{8,5},{9,8},{12,9},{13,12},{3,2},{6,3},{7,6},{10... | collective-permute-start | bytes 3080 | tf_op jit(solution)/shard_map/ppermute | solution.py:20
  152.9 4.6 %collective-permute-start.30 = (f32[2,1,128]{2,1,0:T(1,128)S(1)}, f32[2,1,128]{2,1,0:T(1,128)S(1)}, u32[]{:S(2)}, u32[]{:S(2)}) collective-permute-start(f32[2,1,128]{2,1,0:T(1,128)S(1)} %get-tuple-element.111), channel_id=1, source_target_pairs={{0,1},{1,4},{4,5},{5,8},{8,9},{9,12},{12,13},{2,3},{3,6},{6,7},{7,... | collective-permute-start | bytes 3080 | tf_op jit(solution)/shard_map/ppermute | solution.py:17
  157.8 5.6 %collective-permute-start.31 = (f32[2,1,128]{2,1,0:T(1,128)S(1)}, f32[2,1,128]{2,1,0:T(1,128)S(1)}, u32[]{:S(2)}, u32[]{:S(2)}) collective-permute-start(f32[2,1,128]{2,1,0:T(1,128)S(1)} %get-tuple-element.110), channel_id=1, source_target_pairs={{1,0},{4,1},{5,4},{8,5},{9,8},{12,9},{13,12},{3,2},{6,3},{7,6},{10... | collective-permute-start | bytes 3080 | tf_op jit(solution)/shard_map/ppermute | solution.py:20
  160.0 4.1 %collective-permute-start.32 = (f32[2,1,128]{2,1,0:T(1,128)S(1)}, f32[2,1,128]{2,1,0:T(1,128)S(1)}, u32[]{:S(2)}, u32[]{:S(2)}) collective-permute-start(f32[2,1,128]{2,1,0:T(1,128)S(1)} %get-tuple-element.109), channel_id=1, source_target_pairs={{0,1},{1,4},{4,5},{5,8},{8,9},{9,12},{12,13},{2,3},{3,6},{6,7},{7,... | collective-permute-start | bytes 3080 | tf_op jit(solution)/shard_map/ppermute | solution.py:17
  164.4 6.2 %collective-permute-start.33 = (f32[2,1,128]{2,1,0:T(1,128)S(1)}, f32[2,1,128]{2,1,0:T(1,128)S(1)}, u32[]{:S(2)}, u32[]{:S(2)}) collective-permute-start(f32[2,1,128]{2,1,0:T(1,128)S(1)} %get-tuple-element.108), channel_id=1, source_target_pairs={{1,0},{4,1},{5,4},{8,5},{9,8},{12,9},{13,12},{3,2},{6,3},{7,6},{10... | collective-permute-start | bytes 3080 | tf_op jit(solution)/shard_map/ppermute | solution.py:20
  167.4 3.8 %collective-permute-start.34 = (f32[2,1,128]{2,1,0:T(1,128)S(1)}, f32[2,1,128]{2,1,0:T(1,128)S(1)}, u32[]{:S(2)}, u32[]{:S(2)}) collective-permute-start(f32[2,1,128]{2,1,0:T(1,128)S(1)} %get-tuple-element.107), channel_id=1, source_target_pairs={{0,1},{1,4},{4,5},{5,8},{8,9},{9,12},{12,13},{2,3},{3,6},{6,7},{7,... | collective-permute-start | bytes 3080 | tf_op jit(solution)/shard_map/ppermute | solution.py:17
  171.5 2.1 %copy-start.1 = (f32[4,2,8,128]{3,2,1,0:T(8,128)}, f32[4,2,8,128]{3,2,1,0:T(8,128)S(1)}, u32[]{:S(2)}) copy-start(f32[4,2,8,128]{3,2,1,0:T(8,128)S(1)} %pad_maximum_fusion.28) | copy-start | bytes 98308
where the time goes:
time: 175 us; the launch traced here: 174 us
  starting transfers between devices  100 us (57%)
  local copies, waits for them, and re-layouts  35 us (20%)
  between operations  17.1 us (10%)
  other arithmetic  15.2 us (9%)
  waiting for transfers between devices  6.34 us (4%)
    ppermute x17, starting transfers between devices, extended(): lax.ppermute(lax.slice_in_dim(block, block.shape[dim] - width, None, axis...  58.6 us
    ppermute x17, starting transfers between devices, extended(): lax.ppermute(lax.slice_in_dim(block, 0, width, axis=dim), axis, backward)  40.1 us
    broadcast_in_dim x16, local copies, waits for them, and re-layouts, material_fields(): fields = jnp.where(present, materials[:, zone_no][:, None, None], fields)  21.1 us
    div x16, other arithmetic, advance(): (diagonal * magnet + offdiag * thermal) / determinant  6.68 us
    another operation x1, local copies, waits for them, and re-layouts, restrict(): blocks = values.reshape(shape[:-2] + (shape[-2] // 4, 4, shape[-1] // 4, 4))  5.68 us
  transfers between devices with their start and end apart: 35, of which 7 were waited for; matrix products, arithmetic and copies ran while one was open for 13% of the time, Pallas kernels for 0%

commit v1 on v0

v1 whole, which is shorter than its diff:
```python
import functools
import jax
import jax.numpy as jnp
from jax import lax
from jax.experimental import pallas as pl
from jax.experimental.pallas import tpu as pltpu
from jax.sharding import PartitionSpec as P

JOULE_GAIN = 0.5
MESH = pl.DeviceIdType.MESH
F32 = jnp.float32
BF16 = jnp.bfloat16


def pieces(values):
    high = values.astype(BF16)
    low = (values - high.astype(F32)).astype(BF16)
    return jnp.concatenate([high, low], axis=1)


def advance(sums, turn_amps, keep, mix):
    change = sums[0][1] + turn_amps
    magnet = sums[0][0] + change
    thermal = sums[1][0] + sums[1][1] + JOULE_GAIN * change * change
    return keep * magnet + mix * thermal, mix * magnet + keep * thermal


def link_factors(coupling, span):
    coupled = span * coupling
    diagonal = 1.0 + coupled
    offdiag = 0.5 * coupled
    determinant = diagonal * diagonal - offdiag * offdiag
    return diagonal / determinant, offdiag / determinant


def kernel(
    sizes, starts_hbm, prev_ref, zone_ref, mat_ref, current_ref, bounds_ref,
    gather_ref, spread_ref, ends_ref, new_ref,
    s0, s1, rf, fl, wt, pqs, zt, zb, mu, md, ht, hb, cf, grid_c, tbuf, pbuf, ybuf,
    in_sem, out_sem, send_near, recv_near, send_c, recv_c,
):
    cuts, nsub, tiles, lc, rows, cols, zones, half = sizes
    crow, ccol = rows // 4, cols // 4
    chunks = rows // 8
    cut = lax.axis_index("cuts")
    tile = lax.axis_index("space") * nsub + lax.axis_index("sub")
    has_up = tile > 0
    has_down = tile < tiles - 1
    base = cut * lc

    def where_is(side, cut_no=None):
        other = tile + (side - 1)
        place = {"space": lax.div(other, nsub), "sub": lax.rem(other, nsub)}
        if cut_no is not None:
            place["cuts"] = cut_no
        return place

    def on_side(side):
        if side == 1:
            return lambda fn: fn()
        return pl.when(has_up if side == 0 else has_down)

    load = pltpu.make_async_copy(starts_hbm, s0.at[:, :, pl.ds(8, rows), :], in_sem.at[0])
    load.start()

    barrier = pltpu.get_barrier_semaphore()
    for side in (0, 2):
        @on_side(side)
        def _():
            pl.semaphore_signal(barrier, inc=1, device_id=where_is(side), device_id_type=MESH)
    for step in range(1, cuts):
        other_cut = lax.rem(cut + step, cuts)
        for side in range(3):
            @on_side(side)
            def _():
                pl.semaphore_signal(
                    barrier, inc=1, device_id=where_is(side, other_cut), device_id_type=MESH
                )

    row8 = lax.broadcasted_iota(jnp.int32, (8, cols), 0)
    col8 = lax.broadcasted_iota(jnp.int32, (8, cols), 1)
    rowh = lax.broadcasted_iota(jnp.int32, (2 * half, cols), 0)
    colh = lax.broadcasted_iota(jnp.int32, (2 * half, cols), 1)

    def lookup(zone):
        found = [jnp.full(zone.shape, mat_ref[m, 0], F32) for m in range(4)]
        for zone_no in range(1, zones):
            present = zone == zone_no
            found = [jnp.where(present, mat_ref[m, zone_no], found[m]) for m in range(4)]
        return found

    def restricted(values, buf):
        count = values.shape[0]
        buf[0:count, :] = jnp.dot(
            pieces(values), gather_ref[...], preferred_element_type=F32
        )
        total = buf[pl.ds(0, count // 4, stride=4), :]
        for part in range(1, 4):
            total = total + buf[pl.ds(part, count // 4, stride=4), :]
        return total

    for i in range(chunks):
        found = lookup(zone_ref[8 * i : 8 * i + 8, :])
        for m in range(4):
            fl[m, 8 * i : 8 * i + 8, :] = found[m]
        for m in range(2):
            rf[m, 8 + 8 * i : 16 + 8 * i, :] = found[m]
        keep, mix = link_factors(found[2], 1.0)
        pqs[0, 8 * i : 8 * i + 8, :] = keep
        pqs[1, 8 * i : 8 * i + 8, :] = mix
        pqs[2, 8 * i : 8 * i + 8, :] = found[3]

    load.wait()
    if lc < half:
        mu[...] = jnp.zeros(mu.shape, F32)
        md[...] = jnp.zeros(md.shape, F32)
    for n in range(lc):
        for m in range(2):
            mu[m, half + n : half + n + 1, :] = s0[n, m, 8:9, :]
            mu[m, n : n + 1, :] = s0[n, m, 9:10, :]
            md[m, n : n + 1, :] = s0[n, m, rows + 7 : rows + 8, :]
            md[m, half + n : half + n + 1, :] = s0[n, m, rows + 6 : rows + 7, :]

    ups = jnp.where(has_up, 1, 0) + jnp.where(has_down, 1, 0)
    pl.semaphore_wait(barrier, ups + (cuts - 1) * (1 + ups))

    def near(what, side):
        if what == 0:
            source = zone_ref.at[0:8] if side == 0 else zone_ref.at[rows - 8 : rows]
            target = zb if side == 0 else zt
        elif what == 1:
            source = mu if side == 0 else md
            target = hb if side == 0 else ht
        else:
            source = cf.at[:, pl.ds(crow, crow), :]
            target = cf.at[:, pl.ds(2 * crow if side == 0 else 0, crow), :]
        return pltpu.make_async_remote_copy(
            src_ref=source,
            dst_ref=target,
            send_sem=send_near.at[what, side // 2],
            recv_sem=recv_near.at[what, side // 2],
            device_id=where_is(side),
            device_id_type=MESH,
        )

    def coarse_copy(side, g, local_no, dest):
        return pltpu.make_async_remote_copy(
            src_ref=grid_c.at[g, :, pl.ds(crow, crow), :],
            dst_ref=grid_c.at[g, :, pl.ds((2 - side) * crow, crow), :],
            send_sem=send_c.at[dest, side, local_no],
            recv_sem=recv_c.at[2 - side, g],
            device_id=where_is(side, None if dest == 0 else dest),
            device_id_type=MESH,
        )

    def each_coarse_send(g, local_no, nearby, action):
        for dest in range(1, cuts):
            @pl.when(cut < dest)
            def _():
                for side in (1, 0, 2):
                    @on_side(side)
                    def _():
                        action(coarse_copy(side, g, local_no, dest))
        if nearby:
            for side in (0, 2):
                @on_side(side)
                def _():
                    action(coarse_copy(side, g, local_no, 0))

    def await_coarse(side, g):
        pltpu.make_async_remote_copy(
            src_ref=grid_c.at[g, :, pl.ds(crow, crow), :],
            dst_ref=grid_c.at[g, :, pl.ds(side * crow, crow), :],
            send_sem=send_c.at[0, 0, 0],
            recv_sem=recv_c.at[side, g],
            device_id=where_is(1, lax.rem(cut + 1, cuts)),
            device_id_type=MESH,
        ).wait_recv()

    for what in (0, 1):
        for side in (0, 2):
            @on_side(side)
            def _():
                near(what, side).start()

    @pl.when(jnp.logical_not(has_up))
    def _():
        zt[...] = jnp.zeros(zt.shape, jnp.int32)
        ht[...] = jnp.zeros(ht.shape, F32)
        for m in range(4):
            cf[m, 0:crow, :] = jnp.full((crow, ccol), mat_ref[m, 0], F32)
        grid_c[:, :, 0:crow, :] = jnp.zeros(grid_c.shape[:2] + (crow, ccol), F32)

    @pl.when(jnp.logical_not(has_down))
    def _():
        zb[...] = jnp.zeros(zb.shape, jnp.int32)
        hb[...] = jnp.zeros(hb.shape, F32)
        for m in range(4):
            cf[m, 2 * crow : 3 * crow, :] = jnp.full((crow, ccol), mat_ref[m, 0], F32)
        grid_c[:, :, 2 * crow : 3 * crow, :] = jnp.zeros(grid_c.shape[:2] + (crow, ccol), F32)

    own_c = restricted(fl[...].reshape(4 * rows, cols), tbuf)
    for m in range(4):
        cf[m, crow : 2 * crow, :] = own_c[m * crow : (m + 1) * crow]
    for side in (0, 2):
        @on_side(side)
        def _():
            near(2, side).start()

    @pl.when(cut == 0)
    def _():
        first = restricted(s0[0, :, 8 : 8 + rows, :].reshape(2 * rows, cols), tbuf)
        for m in range(2):
            grid_c[0, m, crow : 2 * crow, :] = first[m * crow : (m + 1) * crow]
        each_coarse_send(0, lc, True, lambda copy: copy.start())

    for side in (0, 2):
        @on_side(side)
        def _():
            near(0, 2 - side).wait_recv()
    above = lookup(zt[...])
    below = lookup(zb[...])
    for m in range(2):
        rf[m, 0:8, :] = above[m]
        rf[m, rows + 8 : rows + 16, :] = below[m]

    def lateral(value, edge, col):
        width = value.shape[1]
        left = jnp.where(col == 0, edge, pltpu.roll(value, 1, 1))
        right = jnp.where(col == width - 1, edge, pltpu.roll(value, width - 1, 1))
        return 0.5 * (value + left), 0.5 * (value + right)

    def five(center, up, down, edge, col):
        west, east = lateral(center, edge, col)
        north = 0.5 * (center + up)
        south = 0.5 * (center + down)
        width = center.shape[1]
        return (
            jnp.where(col == width - 1, 0.0, east),
            jnp.where(col == 0, 0.0, west),
            north,
            south,
            (west + east) + (north + south),
        )

    for m in range(2):
        for i in range(chunks):
            low = 8 + 8 * i
            made = five(
                rf[m, low : low + 8, :], rf[m, low - 1 : low + 7, :],
                rf[m, low + 1 : low + 9, :], mat_ref[m, 0], col8,
            )
            for k in range(5):
                wt[m, k, 8 * i : 8 * i + 8, :] = made[k]

    def spread_sum(weights, center, up, down):
        width = center.shape[1]
        east, west, north, south, whole = weights
        total = east * pltpu.roll(center, width - 1, 1) + west * pltpu.roll(center, 1, 1)
        return (total + (north * up + south * down)) - whole * center

    def amps_at(slice_no, offset):
        return current_ref[bounds_ref[slice_no] + offset].astype(F32) * 0.001

    amps = [[amps_at(base + n, j) for j in range(2)] for n in range(lc)]

    def both(top, bottom):
        shape = (2 * half, cols)
        return jnp.where(rowh < half, jnp.broadcast_to(top, shape), jnp.broadcast_to(bottom, shape))

    edge_weights = []
    for m in range(2):
        center = both(rf[m, 7:8, :], rf[m, rows + 8 : rows + 9, :])
        outer = both(rf[m, 6:7, :], rf[m, rows + 9 : rows + 10, :])
        inner = both(rf[m, 8:9, :], rf[m, rows + 7 : rows + 8, :])
        edge_weights.append(five(center, outer, inner, mat_ref[m, 0], colh))
    edge_keep, edge_mix = link_factors(both(above[2][7:8], below[2][0:1]), 1.0)
    edge_amps = jnp.zeros((2 * half, cols), F32)
    for n in range(lc):
        edge_amps = jnp.where(
            jnp.logical_or(rowh == n, rowh == half + n), amps[n][0], edge_amps
        )
    edge_turn = both(above[3][7:8], below[3][0:1]) * edge_amps

    for side in (0, 2):
        @on_side(side)
        def _():
            near(1, 2 - side).wait_recv()

    edge_sums = []
    for m in range(2):
        center = jnp.where(rowh < half, ht[m], hb[m])
        outer = pltpu.roll(jnp.where(rowh < half, hb[m], ht[m]), half, 0)
        inner = pltpu.roll(jnp.where(rowh < half, md[m], mu[m]), half, 0)
        edge_sums.append((center, spread_sum(edge_weights[m], center, outer, inner)))
        for n in range(lc):
            s0[n, m, 7:8, :] = ht[m, n : n + 1, :]
            s0[n, m, rows + 8 : rows + 9, :] = hb[m, half + n : half + n + 1, :]
    edge_out = advance(edge_sums, edge_turn, edge_keep, edge_mix)
    inside = jnp.where(
        rowh < half, jnp.where(has_up, 1, 0), jnp.where(has_down, 1, 0)
    ) > 0
    for m in range(2):
        kept = jnp.where(inside, edge_out[m], 0.0)
        for n in range(lc):
            s1[n, m, 7:8, :] = kept[n : n + 1]
            s1[n, m, rows + 8 : rows + 9, :] = kept[half + n : half + n + 1]

    def fine_chunk(source, n, i, amperes):
        low = 8 + 8 * i
        at = slice(8 * i, 8 * i + 8)
        sums = []
        for m in range(2):
            center = source[n, m, low : low + 8, :]
            weights = [wt[m, k, at, :] for k in range(5)]
            sums.append((center, spread_sum(
                weights, center, source[n, m, low - 1 : low + 7, :],
                source[n, m, low + 1 : low + 9, :],
            )))
        return advance(sums, pqs[2, at, :] * amperes, pqs[0, at, :], pqs[1, at, :])

    for n in range(lc):
        for i in range(chunks):
            out = fine_chunk(s0, n, i, amps[n][0])
            for m in range(2):
                s1[n, m, 8 + 8 * i : 16 + 8 * i, :] = out[m]
        for i in range(chunks):
            out = fine_chunk(s1, n, i, amps[n][1])
            for m in range(2):
                ends_ref[n, m, 8 * i : 8 * i + 8, :] = out[m]
        mean = restricted(ends_ref[n].reshape(2 * rows, cols), tbuf)
        for m in range(2):
            grid_c[base + n + 1, m, crow : 2 * crow, :] = (
                mean[m * crow : (m + 1) * crow] - prev_ref[n, m]
            )
        each_coarse_send(base + n + 1, n, n < lc - 1, lambda copy: copy.start())

    for side in (0, 2):
        @on_side(side)
        def _():
            near(2, 2 - side).wait_recv()
    tall = 3 * crow
    crows = lax.broadcasted_iota(jnp.int32, (tall, ccol), 0)
    ccols = lax.broadcasted_iota(jnp.int32, (tall, ccol), 1)
    in_grid = jnp.logical_and(
        jnp.where(crows < crow, jnp.where(has_up, 1, 0), 1) > 0,
        jnp.where(crows >= 2 * crow, jnp.where(has_down, 1, 0), 1) > 0,
    )
    coarse_weights = []
    for m in range(2):
        center = cf[m] * 0.125
        coarse_weights.append(five(
            center, pltpu.roll(center, 1, 0), pltpu.roll(center, tall - 1, 0),
            mat_ref[m, 0] * 0.125, ccols,
        ))
    coarse_keep, coarse_mix = link_factors(cf[2], 2.0)
    coarse_turn = 2.0 * cf[3]

    def coarse_step(state, amperes):
        sums = []
        for m in range(2):
            center = state[m]
            sums.append((center, spread_sum(
                coarse_weights[m], center, pltpu.roll(center, 1, 0),
                pltpu.roll(center, tall - 1, 0),
            )))
        return advance(sums, coarse_turn * amperes, coarse_keep, coarse_mix)

    def following(out, g):
        return [jnp.where(in_grid, out[m] + grid_c[g, m], 0.0) for m in range(2)]

    @pl.when(cut > 0)
    def _():
        await_coarse(1, 0)
    for side in (0, 2):
        @on_side(side)
        def _():
            await_coarse(side, 0)
    for m in range(2):
        ybuf[m] = grid_c[0, m]
    for before in range(cuts - 1):
        @pl.when(cut > before)
        def _():
            state = [ybuf[m] for m in range(2)]
            for n in range(lc):
                slice_no = before * lc + n
                out = coarse_step(state, amps_at(slice_no, 0))
                await_coarse(1, slice_no + 1)
                for side in (0, 2):
                    @on_side(side)
                    def _():
                        await_coarse(side, slice_no + 1)
                state = following(out, slice_no + 1)
            for m in range(2):
                ybuf[m] = state[m]

    for n in range(lc - 1):
        for side in (0, 2):
            @on_side(side)
            def _():
                await_coarse(side, base + n + 1)
    state = [ybuf[m] for m in range(2)]
    for n in range(lc):
        out = coarse_step(state, amps[n][0])
        for m in range(2):
            fresh = out[m][crow : 2 * crow]
            new_ref[n, m] = fresh
            gain = fresh - prev_ref[n, m]
            for part in range(4):
                pbuf[n, pl.ds(m * rows + part, crow, stride=4), :] = gain
        if n < lc - 1:
            state = following(out, base + n + 1)
    for n in range(lc):
        added = jnp.dot(pieces(pbuf[n]), spread_ref[...], preferred_element_type=F32)
        ends_ref[n] = ends_ref[n] + added.reshape(2, rows, cols)

    for what in range(3):
        for side in (0, 2):
            @on_side(side)
            def _():
                near(what, side).wait_send()

    @pl.when(cut == 0)
    def _():
        each_coarse_send(0, lc, True, lambda copy: copy.wait_send())
    for n in range(lc):
        each_coarse_send(base + n + 1, n, n < lc - 1, lambda copy: copy.wait_send())


def solution(mesh):
    cuts, nsub = mesh.shape["cuts"], mesh.shape["sub"]
    tiles = mesh.shape["space"] * nsub

    def local(starts, coarse_prev, zone_ids, materials, current, bounds):
        lc, _, rows, cols = starts.shape
        crow, ccol = rows // 4, cols // 4
        half = max(4, lc)
        slices = lc * cuts
        sizes = (cuts, nsub, tiles, lc, rows, cols, materials.shape[1], half)
        match = lax.broadcasted_iota(jnp.int32, (ccol, cols), 1) // 4
        spread = (match == lax.broadcasted_iota(jnp.int32, (ccol, cols), 0)).astype(F32)
        gather = (spread.T * 0.0625).astype(BF16)
        gather = jnp.concatenate([gather, gather], axis=0)
        spread = spread.astype(BF16)
        spread = jnp.concatenate([spread, spread], axis=0)
        vmem = pl.BlockSpec(memory_space=pltpu.VMEM)
        smem = pl.BlockSpec(memory_space=pltpu.SMEM)
        return pl.pallas_call(
            functools.partial(kernel, sizes),
            out_shape=(
                jax.ShapeDtypeStruct(starts.shape, F32),
                jax.ShapeDtypeStruct(coarse_prev.shape, F32),
            ),
            in_specs=[pl.BlockSpec(memory_space=pl.ANY), vmem, vmem, smem, smem, smem, vmem, vmem],
            out_specs=(vmem, vmem),
            scratch_shapes=[
                pltpu.VMEM((lc, 2, rows + 16, cols), F32),
                pltpu.VMEM((lc, 2, rows + 16, cols), F32),
                pltpu.VMEM((2, rows + 16, cols), F32),
                pltpu.VMEM((4, rows, cols), F32),
                pltpu.VMEM((2, 5, rows, cols), F32),
                pltpu.VMEM((3, rows, cols), F32),
                pltpu.VMEM((8, cols), jnp.int32),
                pltpu.VMEM((8, cols), jnp.int32),
                pltpu.VMEM((2, 2 * half, cols), F32),
                pltpu.VMEM((2, 2 * half, cols), F32),
                pltpu.VMEM((2, 2 * half, cols), F32),
                pltpu.VMEM((2, 2 * half, cols), F32),
                pltpu.VMEM((4, 3 * crow, ccol), F32),
                pltpu.VMEM((slices + 1, 2, 3 * crow, ccol), F32),
                pltpu.VMEM((4 * rows, ccol), F32),
                pltpu.VMEM((lc, 2 * rows, ccol), F32),
                pltpu.VMEM((2, 3 * crow, ccol), F32),
                pltpu.SemaphoreType.DMA((1,)),
                pltpu.SemaphoreType.DMA((lc,)),
                pltpu.SemaphoreType.DMA((3, 2)),
                pltpu.SemaphoreType.DMA((3, 2)),
                pltpu.SemaphoreType.DMA((cuts, 3, lc + 1)),
                pltpu.SemaphoreType.DMA((3, slices + 1)),
            ],
            compiler_params=pltpu.CompilerParams(
                collective_id=0, has_side_effects=True, vmem_limit_bytes=32 * 1024 * 1024
            ),
        )(starts, coarse_prev, zone_ids, materials, current, bounds, gather, spread)

    placed = (
        P(("grp", "cuts"), None, ("space", "sub"), None),
        P(("grp", "cuts"), None, ("space", "sub"), None),
        P(("grp", "space", "sub"), None),
        P(),
        P("grp"),
        P(),
    )
    return jax.shard_map(
        local,
        mesh=mesh,
        in_specs=placed,
        out_specs=(
            P(("grp", "cuts"), None, ("space", "sub"), None),
            P(("grp", "cuts"), None, ("space", "sub"), None),
        ),
        check_vma=False,
    )
```

time: 175 us -> 15.3 us (0.09)
  the two profiles are of different devices: /device:TPU:15 before, /device:TPU:1 now
where the time goes in v1:
time: 15.3 us; the launch traced here: 15.2 us
  Pallas kernels  11.9 us (78%)
  local copies, waits for them, and re-layouts  2.24 us (15%)
  between operations  0.73 us (5%)
  other arithmetic  0.35 us (2%)
    pallas_call x1, Pallas kernels, local(): pl.pallas_call(functools.partial(kernel, sizes), out_shape=(jax.ShapeDtyp...  11.9 us
    unnamed x14, local copies, waits for them, and re-layouts  2.24 us

profile of v1, /device:TPU:1, one launch (start us, length us, event | category | flops | bytes accessed | tf_op | source)
XLA Modules:
  0.0 15.2 jit_solution(17275280859848529802)
XLA Ops:
  0.7 0.0 copy-start
  0.7 0.3 %select_convert_fusion = bf16[512,128]{1,0:T(8,128)(2,1)S(1)} fusion(s32[512]{0:T(512)S(1)} %get-tuple-element.2, s32[512]{0:T(512)S(1)} %get-tuple-element.3, pred[512]{0:T(512)(128)(4,1)S(1)} %fusion.2), kind=kLoop, calls=%fused_computation.4 | loop fusion | flops 262144 | bytes 135680 | tf_op jit(solution)/shard_map/convert_element_type | solution.py:442
  1.0 0.0 copy-start.1
  1.0 0.0 copy-start.2
  1.0 0.0 copy-start.3
  1.0 0.0 copy-start.4
  1.1 0.0 copy-start.5
  1.1 0.6 %copy-done = f32[4,2,32,512]{3,2,1,0:T(8,128)S(1)} copy-done((f32[4,2,32,512]{3,2,1,0:T(8,128)S(1)}, f32[4,2,32,512]{3,2,1,0:T(8,128)}, u32[]{:S(2)}) %copy-start) | copy-done | bytes 524312
  1.7 0.2 %copy-done.1 = s32[32,512]{1,0:T(8,128)S(1)} copy-done((s32[32,512]{1,0:T(8,128)S(1)}, s32[32,512]{1,0:T(8,128)}, u32[]{:S(2)}) %copy-start.1) | copy-done | bytes 65560
  1.9 0.0 copy-done.2
  1.9 0.0 copy-done.3
  1.9 0.0 copy-done.4
  1.9 0.0 copy-done.5
  1.9 11.9 %shard_map.77 = (f32[4,2,32,512]{3,2,1,0:T(8,128)S(1)}, f32[4,2,8,128]{3,2,1,0:T(8,128)S(1)}) custom-call(f32[4,2,32,512]{3,2,1,0:T(8,128)S(1)} %copy-done, f32[4,2,8,128]{3,2,1,0:T(8,128)S(1)} %copy-done.2, s32[32,512]{1,0:T(8,128)S(1)} %copy-done.1, f32[4,8]{1,0:T(4,128)S(1)} %copy-done.3, s32[96]{0:T(128)S(1)} %copy-done.4, s32[8]{0:T(128)S(1)} %copy-done.5, ...), custom_call_target="tpu_custom_call" | custom-call | tf_op jit(solution)/shard_map/pallas_call | solution.py:448
  13.8 0.8 %copy.10 = f32[4,2,32,512]{3,2,1,0:T(8,128)} copy(f32[4,2,32,512]{3,2,1,0:T(8,128)S(1)} %get-tuple-element.6) | data formatting | bytes 1048576
  14.6 0.6 %copy.11 = f32[4,2,8,128]{3,2,1,0:T(8,128)} copy(f32[4,2,8,128]{3,2,1,0:T(8,128)S(1)} %get-tuple-element.7) | data formatting | bytes 65536
  (5 shorter events, 0.1 us)
Async XLA Ops:
  0.7 1.0 %copy-start = (f32[4,2,32,512]{3,2,1,0:T(8,128)S(1)}, f32[4,2,32,512]{3,2,1,0:T(8,128)}, u32[]{:S(2)}) copy-start(f32[4,2,32,512]{3,2,1,0:T(8,128)} %starts_hbm.1) | copy-start | bytes 1572868
  1.0 0.9 %copy-start.1 = (s32[32,512]{1,0:T(8,128)S(1)}, s32[32,512]{1,0:T(8,128)}, u32[]{:S(2)}) copy-start(s32[32,512]{1,0:T(8,128)} %zone_ref.1) | copy-start | bytes 196612
  1.0 0.9 %copy-start.2 = (f32[4,2,8,128]{3,2,1,0:T(8,128)S(1)}, f32[4,2,8,128]{3,2,1,0:T(8,128)}, u32[]{:S(2)}) copy-start(f32[4,2,8,128]{3,2,1,0:T(8,128)} %prev_ref.1) | copy-start | bytes 98308
  1.0 0.9 %copy-start.3 = (f32[4,8]{1,0:T(4,128)S(1)}, f32[4,8]{1,0:T(4,128)}, u32[]{:S(2)}) copy-start(f32[4,8]{1,0:T(4,128)} %mat_ref.1) | copy-start | bytes 388
  1.0 0.9 %copy-start.4 = (s32[96]{0:T(128)S(1)}, s32[96]{0:T(128)}, u32[]{:S(2)}) copy-start(s32[96]{0:T(128)} %current_ref.1) | copy-start | bytes 1156
  1.1 0.8 %copy-start.5 = (s32[8]{0:T(128)S(1)}, s32[8]{0:T(128)}, u32[]{:S(2)}) copy-start(s32[8]{0:T(128)} %bounds_ref.1) | copy-start | bytes 100

commit v2 on v1

--- a/solution.py
+++ b/solution.py
@@ -34,10 +34,10 @@
 
 
 def kernel(
-    sizes, starts_hbm, prev_ref, zone_ref, mat_ref, current_ref, bounds_ref,
-    gather_ref, spread_ref, ends_ref, new_ref,
-    s0, s1, rf, fl, wt, pqs, zt, zb, mu, md, ht, hb, cf, grid_c, tbuf, pbuf, ybuf,
-    in_sem, out_sem, send_near, recv_near, send_c, recv_c,
+    sizes, starts_hbm, prev_hbm, zone_hbm, mat_ref, current_ref, bounds_ref,
+    ends_ref, new_ref, pbuf, spread_ref,
+    prev_ref, zone_ref, gather_ref, s0, s1, rf, fl, wt, pqs, zt, zb, mu, md, ht, hb, cf, grid_c, tbuf, ybuf,
+    in_sem, send_near, recv_near, send_c, recv_c,
 ):
     cuts, nsub, tiles, lc, rows, cols, zones, half = sizes
     crow, ccol = rows // 4, cols // 4
@@ -60,8 +60,12 @@
             return lambda fn: fn()
         return pl.when(has_up if side == 0 else has_down)
 
+    load_zone = pltpu.make_async_copy(zone_hbm, zone_ref, in_sem.at[1])
+    load_zone.start()
     load = pltpu.make_async_copy(starts_hbm, s0.at[:, :, pl.ds(8, rows), :], in_sem.at[0])
     load.start()
+    load_prev = pltpu.make_async_copy(prev_hbm, prev_ref, in_sem.at[2])
+    load_prev.start()
 
     barrier = pltpu.get_barrier_semaphore()
     for side in (0, 2):
@@ -99,6 +103,17 @@
             total = total + buf[pl.ds(part, count // 4, stride=4), :]
         return total
 
+    tall_row = lax.broadcasted_iota(jnp.int32, (cols, ccol), 0)
+    tall_col = lax.broadcasted_iota(jnp.int32, (cols, ccol), 1)
+    wide_row = lax.broadcasted_iota(jnp.int32, (ccol, cols), 0)
+    wide_col = lax.broadcasted_iota(jnp.int32, (ccol, cols), 1)
+    gather = jnp.where((tall_row >> 2) == tall_col, 0.0625, 0.0).astype(BF16)
+    spread = jnp.where((wide_col >> 2) == wide_row, 1.0, 0.0).astype(BF16)
+    for part in range(2):
+        gather_ref[part * cols : (part + 1) * cols, :] = gather
+        spread_ref[part * ccol : (part + 1) * ccol, :] = spread
+
+    load_zone.wait()
     for i in range(chunks):
         found = lookup(zone_ref[8 * i : 8 * i + 8, :])
         for m in range(4):
@@ -214,16 +229,6 @@
             grid_c[0, m, crow : 2 * crow, :] = first[m * crow : (m + 1) * crow]
         each_coarse_send(0, lc, True, lambda copy: copy.start())
 
-    for side in (0, 2):
-        @on_side(side)
-        def _():
-            near(0, 2 - side).wait_recv()
-    above = lookup(zt[...])
-    below = lookup(zb[...])
-    for m in range(2):
-        rf[m, 0:8, :] = above[m]
-        rf[m, rows + 8 : rows + 16, :] = below[m]
-
     def lateral(value, edge, col):
         width = value.shape[1]
         left = jnp.where(col == 0, edge, pltpu.roll(value, 1, 1))
@@ -243,9 +248,9 @@
             (west + east) + (north + south),
         )
 
-    for m in range(2):
-        for i in range(chunks):
-            low = 8 + 8 * i
+    def make_weights(i):
+        low = 8 + 8 * i
+        for m in range(2):
             made = five(
                 rf[m, low : low + 8, :], rf[m, low - 1 : low + 7, :],
                 rf[m, low + 1 : low + 9, :], mat_ref[m, 0], col8,
@@ -263,6 +268,43 @@
         return current_ref[bounds_ref[slice_no] + offset].astype(F32) * 0.001
 
     amps = [[amps_at(base + n, j) for j in range(2)] for n in range(lc)]
+
+    def fine_chunk(source, n, i, amperes):
+        low = 8 + 8 * i
+        at = slice(8 * i, 8 * i + 8)
+        sums = []
+        for m in range(2):
+            center = source[n, m, low : low + 8, :]
+            weights = [wt[m, k, at, :] for k in range(5)]
+            sums.append((center, spread_sum(
+                weights, center, source[n, m, low - 1 : low + 7, :],
+                source[n, m, low + 1 : low + 9, :],
+            )))
+        return advance(sums, pqs[2, at, :] * amperes, pqs[0, at, :], pqs[1, at, :])
+
+    def first_step(n, i):
+        out = fine_chunk(s0, n, i, amps[n][0])
+        for m in range(2):
+            s1[n, m, 8 + 8 * i : 16 + 8 * i, :] = out[m]
+
+    for i in range(1, chunks - 1):
+        make_weights(i)
+    for n in range(lc):
+        for i in range(1, chunks - 1):
+            first_step(n, i)
+
+    for side in (0, 2):
+        @on_side(side)
+        def _():
+            near(0, 2 - side).wait_recv()
+    above = lookup(zt[...])
+    below = lookup(zb[...])
+    for m in range(2):
+        rf[m, 0:8, :] = above[m]
+        rf[m, rows + 8 : rows + 16, :] = below[m]
+
+    for i in (0, chunks - 1):
+        make_weights(i)
 
     def both(top, bottom):
         shape = (2 * half, cols)
@@ -306,24 +348,10 @@
             s1[n, m, 7:8, :] = kept[n : n + 1]
             s1[n, m, rows + 8 : rows + 9, :] = kept[half + n : half + n + 1]
 
-    def fine_chunk(source, n, i, amperes):
-        low = 8 + 8 * i
-        at = slice(8 * i, 8 * i + 8)
-        sums = []
-        for m in range(2):
-            center = source[n, m, low : low + 8, :]
-            weights = [wt[m, k, at, :] for k in range(5)]
-            sums.append((center, spread_sum(
-                weights, center, source[n, m, low - 1 : low + 7, :],
-                source[n, m, low + 1 : low + 9, :],
-            )))
-        return advance(sums, pqs[2, at, :] * amperes, pqs[0, at, :], pqs[1, at, :])
-
-    for n in range(lc):
-        for i in range(chunks):
-            out = fine_chunk(s0, n, i, amps[n][0])
-            for m in range(2):
-                s1[n, m, 8 + 8 * i : 16 + 8 * i, :] = out[m]
+    load_prev.wait()
+    for n in range(lc):
+        for i in (0, chunks - 1):
+            first_step(n, i)
         for i in range(chunks):
             out = fine_chunk(s1, n, i, amps[n][1])
             for m in range(2):
@@ -410,9 +438,6 @@
                 pbuf[n, pl.ds(m * rows + part, crow, stride=4), :] = gain
         if n < lc - 1:
             state = following(out, base + n + 1)
-    for n in range(lc):
-        added = jnp.dot(pieces(pbuf[n]), spread_ref[...], preferred_element_type=F32)
-        ends_ref[n] = ends_ref[n] + added.reshape(2, rows, cols)
 
     for what in range(3):
         for side in (0, 2):
@@ -425,6 +450,19 @@
         each_coarse_send(0, lc, True, lambda copy: copy.wait_send())
     for n in range(lc):
         each_coarse_send(base + n + 1, n, n < lc - 1, lambda copy: copy.wait_send())
+
+
+def finish(fine_ref, new_ref, pbuf, spread_ref, ends_out, new_out, total, sems):
+    lc, _, rows, cols = fine_ref.shape
+    copies = [pltpu.make_async_copy(new_ref, new_out, sems.at[lc])]
+    copies[0].start()
+    for n in range(lc):
+        added = jnp.dot(pieces(pbuf[n]), spread_ref[...], preferred_element_type=F32)
+        total[n] = fine_ref[n] + added.reshape(2, rows, cols)
+        copies.append(pltpu.make_async_copy(total.at[n], ends_out.at[n], sems.at[n]))
+        copies[-1].start()
+    for copy in copies:
+        copy.wait()
 
 
 def solution(mesh):
@@ -437,23 +475,23 @@
         half = max(4, lc)
         slices = lc * cuts
         sizes = (cuts, nsub, tiles, lc, rows, cols, materials.shape[1], half)
-        match = lax.broadcasted_iota(jnp.int32, (ccol, cols), 1) // 4
-        spread = (match == lax.broadcasted_iota(jnp.int32, (ccol, cols), 0)).astype(F32)
-        gather = (spread.T * 0.0625).astype(BF16)
-        gather = jnp.concatenate([gather, gather], axis=0)
-        spread = spread.astype(BF16)
-        spread = jnp.concatenate([spread, spread], axis=0)
         vmem = pl.BlockSpec(memory_space=pltpu.VMEM)
         smem = pl.BlockSpec(memory_space=pltpu.SMEM)
-        return pl.pallas_call(
+        hbm = pl.BlockSpec(memory_space=pltpu.HBM)
+        fine, new, risen, spread = pl.pallas_call(
             functools.partial(kernel, sizes),
             out_shape=(
                 jax.ShapeDtypeStruct(starts.shape, F32),
                 jax.ShapeDtypeStruct(coarse_prev.shape, F32),
+                jax.ShapeDtypeStruct((lc, 2 * rows, ccol), F32),
+                jax.ShapeDtypeStruct((2 * ccol, cols), BF16),
             ),
-            in_specs=[pl.BlockSpec(memory_space=pl.ANY), vmem, vmem, smem, smem, smem, vmem, vmem],
-            out_specs=(vmem, vmem),
+            in_specs=[hbm, hbm, hbm, smem, smem, smem],
+            out_specs=(vmem,) * 4,
             scratch_shapes=[
+                pltpu.VMEM((lc, 2, crow, ccol), F32),
+                pltpu.VMEM((rows, cols), jnp.int32),
+                pltpu.VMEM((2 * cols, ccol), BF16),
                 pltpu.VMEM((lc, 2, rows + 16, cols), F32),
                 pltpu.VMEM((lc, 2, rows + 16, cols), F32),
                 pltpu.VMEM((2, rows + 16, cols), F32),
@@ -469,10 +507,8 @@
                 pltpu.VMEM((4, 3 * crow, ccol), F32),
                 pltpu.VMEM((slices + 1, 2, 3 * crow, ccol), F32),
                 pltpu.VMEM((4 * rows, ccol), F32),
-                pltpu.VMEM((lc, 2 * rows, ccol), F32),
                 pltpu.VMEM((2, 3 * crow, ccol), F32),
-                pltpu.SemaphoreType.DMA((1,)),
-                pltpu.SemaphoreType.DMA((lc,)),
+                pltpu.SemaphoreType.DMA((3,)),
                 pltpu.SemaphoreType.DMA((3, 2)),
                 pltpu.SemaphoreType.DMA((3, 2)),
                 pltpu.SemaphoreType.DMA((cuts, 3, lc + 1)),
@@ -481,7 +517,21 @@
             compiler_params=pltpu.CompilerParams(
                 collective_id=0, has_side_effects=True, vmem_limit_bytes=32 * 1024 * 1024
             ),
-        )(starts, coarse_prev, zone_ids, materials, current, bounds, gather, spread)
+        )(starts, coarse_prev, zone_ids, materials, current, bounds)
+        return pl.pallas_call(
+            finish,
+            out_shape=(
+                jax.ShapeDtypeStruct(starts.shape, F32),
+                jax.ShapeDtypeStruct(coarse_prev.shape, F32),
+            ),
+            in_specs=[vmem] * 4,
+            out_specs=(hbm, hbm),
+            scratch_shapes=[
+                pltpu.VMEM(starts.shape, F32),
+                pltpu.SemaphoreType.DMA((lc + 1,)),
+            ],
+            compiler_params=pltpu.CompilerParams(vmem_limit_bytes=16 * 1024 * 1024),
+        )(fine, new, risen, spread)
 
     placed = (
         P(("grp", "cuts"), None, ("space", "sub"), None),

time: 15.3 us -> 18.3 us (1.20)
  local copies, waits for them, and re-layouts: 2.24 us -> 4.62 us
  Pallas kernels: 11.9 us -> 12.7 us
  other arithmetic: 0.35 us -> 0 us
    unnamed x14 -> x12, local copies, waits for them, and re-layouts: 2.24 us -> 4.62 us
    pallas_call x0 -> x1, Pallas kernels: none -> 1.03 us  [local(): pl.pallas_call(finish, out_shape=(jax.ShapeDtypeStruct(starts.shape, F32)...]
    convert_element_type x2 -> x0, other arithmetic: 0.3 us -> none  [the longest x1 0.27 us: local(): gather = (spread.T * 0.0625).astype(BF16)]
where the time goes in v2:
time: 18.3 us; the launch traced here: 18 us
  Pallas kernels  12.7 us (69%)
  local copies, waits for them, and re-layouts  4.62 us (25%)
  between operations  0.65 us (4%)
    pallas_call x1, Pallas kernels, local(): pl.pallas_call(functools.partial(kernel, sizes), out_shape=(jax.ShapeDtyp...  11.7 us
    unnamed x12, local copies, waits for them, and re-layouts  4.62 us
    pallas_call x1, Pallas kernels, local(): pl.pallas_call(finish, out_shape=(jax.ShapeDtypeStruct(starts.shape, F32)...  1.03 us

profile of v2, /device:TPU:1, one launch (start us, length us, event | category | flops | bytes accessed | tf_op | source)
XLA Modules:
  0.0 18.0 jit_solution(3016363956534714417)
XLA Ops:
  0.6 0.0 copy-start
  0.6 1.0 %copy-done = f32[4,2,32,512]{3,2,1,0:T(8,128)S(1)} copy-done((f32[4,2,32,512]{3,2,1,0:T(8,128)S(1)}, f32[4,2,32,512]{3,2,1,0:T(8,128)}, u32[]{:S(2)}) %copy-start) | copy-done | bytes 524312
  1.7 0.0 copy-start.1
  1.7 0.8 %copy-done.1 = s32[32,512]{1,0:T(8,128)S(1)} copy-done((s32[32,512]{1,0:T(8,128)S(1)}, s32[32,512]{1,0:T(8,128)}, u32[]{:S(2)}) %copy-start.1) | copy-done | bytes 65560
  2.5 0.0 copy-start.2
  2.5 0.8 %copy-done.2 = f32[4,2,8,128]{3,2,1,0:T(8,128)S(1)} copy-done((f32[4,2,8,128]{3,2,1,0:T(8,128)S(1)}, f32[4,2,8,128]{3,2,1,0:T(8,128)}, u32[]{:S(2)}) %copy-start.2) | copy-done | bytes 32792
  3.3 0.0 copy-start.3
  3.3 0.7 %copy-done.3 = f32[4,8]{1,0:T(4,128)S(1)} copy-done((f32[4,8]{1,0:T(4,128)S(1)}, f32[4,8]{1,0:T(4,128)}, u32[]{:S(2)}) %copy-start.3) | copy-done | bytes 152
  4.0 0.0 copy-start.4
  4.0 0.7 %copy-done.4 = s32[96]{0:T(128)S(1)} copy-done((s32[96]{0:T(128)S(1)}, s32[96]{0:T(128)}, u32[]{:S(2)}) %copy-start.4) | copy-done | bytes 408
  4.6 0.0 copy-start.5
  4.6 0.7 %copy-done.5 = s32[8]{0:T(128)S(1)} copy-done((s32[8]{0:T(128)S(1)}, s32[8]{0:T(128)}, u32[]{:S(2)}) %copy-start.5) | copy-done | bytes 56
  5.3 11.7 %shard_map.77 = (f32[4,2,32,512]{3,2,1,0:T(8,128)S(1)}, f32[4,2,8,128]{3,2,1,0:T(8,128)S(1)}, f32[4,64,128]{2,1,0:T(8,128)S(1)}, bf16[256,512]{1,0:T(8,128)(2,1)S(1)}) custom-call(f32[4,2,32,512]{3,2,1,0:T(8,128)S(1)} %copy-done, f32[4,2,8,128]{3,2,1,0:T(8,128)S(1)} %copy-done.2, s32[32,512]{1,0:T(8,128)S(1)} %copy-done.1, f32[4,8]{1,0:T(4,128)S(1)} %copy-done.3, ...), custom_call_target="tpu_custom_call" | custom-call | tf_op jit(solution)/shard_map/pallas_call | solution.py:481
  17.0 1.0 %shard_map.78 = (f32[4,2,32,512]{3,2,1,0:T(8,128)}, f32[4,2,8,128]{3,2,1,0:T(8,128)}) custom-call(f32[4,2,32,512]{3,2,1,0:T(8,128)S(1)} %get-tuple-element.6.fine_ref, f32[4,2,8,128]{3,2,1,0:T(8,128)S(1)} %get-tuple-element.7.new_ref, f32[4,64,128]{2,1,0:T(8,128)S(1)} %get-tuple-element.8.pbuf, bf16[256,512]{1,0:T(8,128)(2,1)S(1)} %get-tuple-element.9.spread_ref), custom_call_target="tpu_custom_call" | custom-call | tf_op jit(solution)/shard_map/pallas_call | solution.py:521
Async XLA Ops:
  0.6 1.0 %copy-start = (f32[4,2,32,512]{3,2,1,0:T(8,128)S(1)}, f32[4,2,32,512]{3,2,1,0:T(8,128)}, u32[]{:S(2)}) copy-start(f32[4,2,32,512]{3,2,1,0:T(8,128)} %starts_hbm.1) | copy-start | bytes 1572868
  1.7 0.8 %copy-start.1 = (s32[32,512]{1,0:T(8,128)S(1)}, s32[32,512]{1,0:T(8,128)}, u32[]{:S(2)}) copy-start(s32[32,512]{1,0:T(8,128)} %zone_hbm.1) | copy-start | bytes 196612
  2.5 0.8 %copy-start.2 = (f32[4,2,8,128]{3,2,1,0:T(8,128)S(1)}, f32[4,2,8,128]{3,2,1,0:T(8,128)}, u32[]{:S(2)}) copy-start(f32[4,2,8,128]{3,2,1,0:T(8,128)} %prev_hbm.1) | copy-start | bytes 98308
  3.3 0.7 %copy-start.3 = (f32[4,8]{1,0:T(4,128)S(1)}, f32[4,8]{1,0:T(4,128)}, u32[]{:S(2)}) copy-start(f32[4,8]{1,0:T(4,128)} %mat_ref.1) | copy-start | bytes 388
  4.0 0.7 %copy-start.4 = (s32[96]{0:T(128)S(1)}, s32[96]{0:T(128)}, u32[]{:S(2)}) copy-start(s32[96]{0:T(128)} %current_ref.1) | copy-start | bytes 1156
  4.6 0.7 %copy-start.5 = (s32[8]{0:T(128)S(1)}, s32[8]{0:T(128)}, u32[]{:S(2)}) copy-start(s32[8]{0:T(128)} %bounds_ref.1) | copy-start | bytes 100

commit v3 on v2

--- a/solution.py
+++ b/solution.py
@@ -34,9 +34,9 @@
 
 
 def kernel(
-    sizes, starts_hbm, prev_hbm, zone_hbm, mat_ref, current_ref, bounds_ref,
+    sizes, starts_hbm, prev_hbm, zone_hbm, mat_hbm, current_hbm, bounds_hbm,
     ends_ref, new_ref, pbuf, spread_ref,
-    prev_ref, zone_ref, gather_ref, s0, s1, rf, fl, wt, pqs, zt, zb, mu, md, ht, hb, cf, grid_c, tbuf, ybuf,
+    mat_ref, current_ref, bounds_ref, prev_ref, zone_ref, gather_ref, s0, s1, rf, fl, wt, pqs, zt, zb, mu, md, ht, hb, cf, grid_c, tbuf, ybuf,
     in_sem, send_near, recv_near, send_c, recv_c,
 ):
     cuts, nsub, tiles, lc, rows, cols, zones, half = sizes
@@ -62,6 +62,14 @@
 
     load_zone = pltpu.make_async_copy(zone_hbm, zone_ref, in_sem.at[1])
     load_zone.start()
+    small = [
+        pltpu.make_async_copy(source, target, in_sem.at[3 + k])
+        for k, (source, target) in enumerate(
+            ((mat_hbm, mat_ref), (current_hbm, current_ref), (bounds_hbm, bounds_ref))
+        )
+    ]
+    for copy in small:
+        copy.start()
     load = pltpu.make_async_copy(starts_hbm, s0.at[:, :, pl.ds(8, rows), :], in_sem.at[0])
     load.start()
     load_prev = pltpu.make_async_copy(prev_hbm, prev_ref, in_sem.at[2])
@@ -113,6 +121,8 @@
         gather_ref[part * cols : (part + 1) * cols, :] = gather
         spread_ref[part * ccol : (part + 1) * ccol, :] = spread
 
+    for copy in small:
+        copy.wait()
     load_zone.wait()
     for i in range(chunks):
         found = lookup(zone_ref[8 * i : 8 * i + 8, :])
@@ -476,7 +486,6 @@
         slices = lc * cuts
         sizes = (cuts, nsub, tiles, lc, rows, cols, materials.shape[1], half)
         vmem = pl.BlockSpec(memory_space=pltpu.VMEM)
-        smem = pl.BlockSpec(memory_space=pltpu.SMEM)
         hbm = pl.BlockSpec(memory_space=pltpu.HBM)
         fine, new, risen, spread = pl.pallas_call(
             functools.partial(kernel, sizes),
@@ -486,9 +495,12 @@
                 jax.ShapeDtypeStruct((lc, 2 * rows, ccol), F32),
                 jax.ShapeDtypeStruct((2 * ccol, cols), BF16),
             ),
-            in_specs=[hbm, hbm, hbm, smem, smem, smem],
+            in_specs=[hbm] * 6,
             out_specs=(vmem,) * 4,
             scratch_shapes=[
+                pltpu.SMEM(materials.shape, F32),
+                pltpu.SMEM(current.shape, jnp.int32),
+                pltpu.SMEM(bounds.shape, jnp.int32),
                 pltpu.VMEM((lc, 2, crow, ccol), F32),
                 pltpu.VMEM((rows, cols), jnp.int32),
                 pltpu.VMEM((2 * cols, ccol), BF16),
@@ -508,7 +520,7 @@
                 pltpu.VMEM((slices + 1, 2, 3 * crow, ccol), F32),
                 pltpu.VMEM((4 * rows, ccol), F32),
                 pltpu.VMEM((2, 3 * crow, ccol), F32),
-                pltpu.SemaphoreType.DMA((3,)),
+                pltpu.SemaphoreType.DMA((6,)),
                 pltpu.SemaphoreType.DMA((3, 2)),
                 pltpu.SemaphoreType.DMA((3, 2)),
                 pltpu.SemaphoreType.DMA((cuts, 3, lc + 1)),
@@ -517,7 +529,10 @@
             compiler_params=pltpu.CompilerParams(
                 collective_id=0, has_side_effects=True, vmem_limit_bytes=32 * 1024 * 1024
             ),
-        )(starts, coarse_prev, zone_ids, materials, current, bounds)
+        )(*(
+            pltpu.with_memory_space_constraint(given, pltpu.HBM)
+            for given in (starts, coarse_prev, zone_ids, materials, current, bounds)
+        ))
         return pl.pallas_call(
             finish,
             out_shape=(

time: 18.3 us -> 12.8 us (0.70)
  local copies, waits for them, and re-layouts: 4.62 us -> 0 us
  Pallas kernels: 12.7 us -> 12 us
    unnamed x12 -> x0, local copies, waits for them, and re-layouts: 4.62 us -> none
    pallas_call x1, Pallas kernels: 11.7 us -> 11 us  [local(): pl.pallas_call(functools.partial(kernel, sizes), out_shape=(jax.ShapeDtyp...]
where the time goes in v3:
time: 12.8 us; the launch traced here: 12.7 us
  Pallas kernels  12 us (94%)
  between operations  0.64 us (5%)
    pallas_call x1, Pallas kernels, local(): pl.pallas_call(functools.partial(kernel, sizes), out_shape=(jax.ShapeDtyp...  11 us
    pallas_call x1, Pallas kernels, local(): pl.pallas_call(finish, out_shape=(jax.ShapeDtypeStruct(starts.shape, F32)...  1.03 us

profile of v3, /device:TPU:1, one launch (start us, length us, event | category | flops | bytes accessed | tf_op | source)
XLA Modules:
  0.0 12.7 jit_solution(16485837106138784185)
XLA Ops:
  0.6 11.0 %shard_map.77 = (f32[4,2,32,512]{3,2,1,0:T(8,128)S(1)}, f32[4,2,8,128]{3,2,1,0:T(8,128)S(1)}, f32[4,64,128]{2,1,0:T(8,128)S(1)}, bf16[256,512]{1,0:T(8,128)(2,1)S(1)}) custom-call(f32[4,2,32,512]{3,2,1,0:T(8,128)} %starts_hbm.1, f32[4,2,8,128]{3,2,1,0:T(8,128)} %prev_hbm.1, s32[32,512]{1,0:T(8,128)} %zone_hbm.1, f32[4,8]{1,0:T(4,128)} %mat_hbm.1, ...), custom_call_target="tpu_custom_call" | custom-call | tf_op jit(solution)/shard_map/pallas_call | solution.py:490
  11.6 1.0 %shard_map.78 = (f32[4,2,32,512]{3,2,1,0:T(8,128)}, f32[4,2,8,128]{3,2,1,0:T(8,128)}) custom-call(f32[4,2,32,512]{3,2,1,0:T(8,128)S(1)} %get-tuple-element.6.fine_ref, f32[4,2,8,128]{3,2,1,0:T(8,128)S(1)} %get-tuple-element.7.new_ref, f32[4,64,128]{2,1,0:T(8,128)S(1)} %get-tuple-element.8.pbuf, bf16[256,512]{1,0:T(8,128)(2,1)S(1)} %get-tuple-element.9.spread_ref), custom_call_target="tpu_custom_call" | custom-call | tf_op jit(solution)/shard_map/pallas_call | solution.py:536

commit v4 on v3

--- a/solution.py
+++ b/solution.py
@@ -60,8 +60,6 @@
             return lambda fn: fn()
         return pl.when(has_up if side == 0 else has_down)
 
-    load_zone = pltpu.make_async_copy(zone_hbm, zone_ref, in_sem.at[1])
-    load_zone.start()
     small = [
         pltpu.make_async_copy(source, target, in_sem.at[3 + k])
         for k, (source, target) in enumerate(
@@ -70,8 +68,18 @@
     ]
     for copy in small:
         copy.start()
-    load = pltpu.make_async_copy(starts_hbm, s0.at[:, :, pl.ds(8, rows), :], in_sem.at[0])
-    load.start()
+    loads = [
+        pltpu.make_async_copy(
+            starts_hbm.at[:, :, pl.ds(first, count), :],
+            s0.at[:, :, pl.ds(8 + first, count), :],
+            in_sem.at[place],
+        )
+        for first, count, place in ((0, 8, 0), (rows - 8, 8, 6), (8, rows - 16, 7))
+    ]
+    for copy in loads:
+        copy.start()
+    load_zone = pltpu.make_async_copy(zone_hbm, zone_ref, in_sem.at[1])
+    load_zone.start()
     load_prev = pltpu.make_async_copy(prev_hbm, prev_ref, in_sem.at[2])
     load_prev.start()
 
@@ -111,31 +119,8 @@
             total = total + buf[pl.ds(part, count // 4, stride=4), :]
         return total
 
-    tall_row = lax.broadcasted_iota(jnp.int32, (cols, ccol), 0)
-    tall_col = lax.broadcasted_iota(jnp.int32, (cols, ccol), 1)
-    wide_row = lax.broadcasted_iota(jnp.int32, (ccol, cols), 0)
-    wide_col = lax.broadcasted_iota(jnp.int32, (ccol, cols), 1)
-    gather = jnp.where((tall_row >> 2) == tall_col, 0.0625, 0.0).astype(BF16)
-    spread = jnp.where((wide_col >> 2) == wide_row, 1.0, 0.0).astype(BF16)
-    for part in range(2):
-        gather_ref[part * cols : (part + 1) * cols, :] = gather
-        spread_ref[part * ccol : (part + 1) * ccol, :] = spread
-
-    for copy in small:
-        copy.wait()
-    load_zone.wait()
-    for i in range(chunks):
-        found = lookup(zone_ref[8 * i : 8 * i + 8, :])
-        for m in range(4):
-            fl[m, 8 * i : 8 * i + 8, :] = found[m]
-        for m in range(2):
-            rf[m, 8 + 8 * i : 16 + 8 * i, :] = found[m]
-        keep, mix = link_factors(found[2], 1.0)
-        pqs[0, 8 * i : 8 * i + 8, :] = keep
-        pqs[1, 8 * i : 8 * i + 8, :] = mix
-        pqs[2, 8 * i : 8 * i + 8, :] = found[3]
-
-    load.wait()
+    loads[0].wait()
+    loads[1].wait()
     if lc < half:
         mu[...] = jnp.zeros(mu.shape, F32)
         md[...] = jnp.zeros(md.shape, F32)
@@ -151,7 +136,7 @@
 
     def near(what, side):
         if what == 0:
-            source = zone_ref.at[0:8] if side == 0 else zone_ref.at[rows - 8 : rows]
+            source = zone_hbm.at[0:8] if side == 0 else zone_hbm.at[rows - 8 : rows]
             target = zb if side == 0 else zt
         elif what == 1:
             source = mu if side == 0 else md
@@ -168,36 +153,35 @@
             device_id_type=MESH,
         )
 
-    def coarse_copy(side, g, local_no, dest):
+    def coarse_copy(side, first, count, mark, kind, dest):
         return pltpu.make_async_remote_copy(
-            src_ref=grid_c.at[g, :, pl.ds(crow, crow), :],
-            dst_ref=grid_c.at[g, :, pl.ds((2 - side) * crow, crow), :],
-            send_sem=send_c.at[dest, side, local_no],
-            recv_sem=recv_c.at[2 - side, g],
+            src_ref=grid_c.at[pl.ds(first, count), :, pl.ds(crow, crow), :],
+            dst_ref=grid_c.at[pl.ds(first, count), :, pl.ds((2 - side) * crow, crow), :],
+            send_sem=send_c.at[dest, side, kind],
+            recv_sem=recv_c.at[2 - side, mark],
             device_id=where_is(side, None if dest == 0 else dest),
             device_id_type=MESH,
         )
 
-    def each_coarse_send(g, local_no, nearby, action):
+    def each_coarse_send(first, count, mark, kind, action):
+        for side in (0, 2):
+            @on_side(side)
+            def _():
+                action(coarse_copy(side, first, count, mark, kind, 0))
         for dest in range(1, cuts):
             @pl.when(cut < dest)
             def _():
                 for side in (1, 0, 2):
                     @on_side(side)
                     def _():
-                        action(coarse_copy(side, g, local_no, dest))
-        if nearby:
-            for side in (0, 2):
-                @on_side(side)
-                def _():
-                    action(coarse_copy(side, g, local_no, 0))
-
-    def await_coarse(side, g):
+                        action(coarse_copy(side, first, count, mark, kind, dest))
+
+    def await_coarse(side, first, count, mark):
         pltpu.make_async_remote_copy(
-            src_ref=grid_c.at[g, :, pl.ds(crow, crow), :],
-            dst_ref=grid_c.at[g, :, pl.ds(side * crow, crow), :],
+            src_ref=grid_c.at[pl.ds(first, count), :, pl.ds(crow, crow), :],
+            dst_ref=grid_c.at[pl.ds(first, count), :, pl.ds(side * crow, crow), :],
             send_sem=send_c.at[0, 0, 0],
-            recv_sem=recv_c.at[side, g],
+            recv_sem=recv_c.at[side, mark],
             device_id=where_is(1, lax.rem(cut + 1, cuts)),
             device_id_type=MESH,
         ).wait_recv()
@@ -207,6 +191,8 @@
             @on_side(side)
             def _():
                 near(what, side).start()
+    for copy in small:
+        copy.wait()
 
     @pl.when(jnp.logical_not(has_up))
     def _():
@@ -224,6 +210,28 @@
             cf[m, 2 * crow : 3 * crow, :] = jnp.full((crow, ccol), mat_ref[m, 0], F32)
         grid_c[:, :, 2 * crow : 3 * crow, :] = jnp.zeros(grid_c.shape[:2] + (crow, ccol), F32)
 
+    tall_row = lax.broadcasted_iota(jnp.int32, (cols, ccol), 0)
+    tall_col = lax.broadcasted_iota(jnp.int32, (cols, ccol), 1)
+    wide_row = lax.broadcasted_iota(jnp.int32, (ccol, cols), 0)
+    wide_col = lax.broadcasted_iota(jnp.int32, (ccol, cols), 1)
+    gather = jnp.where((tall_row >> 2) == tall_col, 0.0625, 0.0).astype(BF16)
+    spread = jnp.where((wide_col >> 2) == wide_row, 1.0, 0.0).astype(BF16)
+    for part in range(2):
+        gather_ref[part * cols : (part + 1) * cols, :] = gather
+        spread_ref[part * ccol : (part + 1) * ccol, :] = spread
+
+    load_zone.wait()
+    for i in range(chunks):
+        found = lookup(zone_ref[8 * i : 8 * i + 8, :])
+        for m in range(4):
+            fl[m, 8 * i : 8 * i + 8, :] = found[m]
+        for m in range(2):
+            rf[m, 8 + 8 * i : 16 + 8 * i, :] = found[m]
+        keep, mix = link_factors(found[2], 1.0)
+        pqs[0, 8 * i : 8 * i + 8, :] = keep
+        pqs[1, 8 * i : 8 * i + 8, :] = mix
+        pqs[2, 8 * i : 8 * i + 8, :] = found[3]
+
     own_c = restricted(fl[...].reshape(4 * rows, cols), tbuf)
     for m in range(4):
         cf[m, crow : 2 * crow, :] = own_c[m * crow : (m + 1) * crow]
@@ -232,12 +240,14 @@
         def _():
             near(2, side).start()
 
+    loads[2].wait()
+
     @pl.when(cut == 0)
     def _():
         first = restricted(s0[0, :, 8 : 8 + rows, :].reshape(2 * rows, cols), tbuf)
         for m in range(2):
             grid_c[0, m, crow : 2 * crow, :] = first[m * crow : (m + 1) * crow]
-        each_coarse_send(0, lc, True, lambda copy: copy.start())
+        each_coarse_send(0, 1, 0, 0, lambda copy: copy.start())
 
     def lateral(value, edge, col):
         width = value.shape[1]
@@ -371,7 +381,7 @@
             grid_c[base + n + 1, m, crow : 2 * crow, :] = (
                 mean[m * crow : (m + 1) * crow] - prev_ref[n, m]
             )
-        each_coarse_send(base + n + 1, n, n < lc - 1, lambda copy: copy.start())
+    each_coarse_send(base + 1, lc, cut + 1, 1, lambda copy: copy.start())
 
     for side in (0, 2):
         @on_side(side)
@@ -409,34 +419,32 @@
 
     @pl.when(cut > 0)
     def _():
-        await_coarse(1, 0)
-    for side in (0, 2):
-        @on_side(side)
-        def _():
-            await_coarse(side, 0)
+        await_coarse(1, 0, 1, 0)
+    for side in (0, 2):
+        @on_side(side)
+        def _():
+            await_coarse(side, 0, 1, 0)
     for m in range(2):
         ybuf[m] = grid_c[0, m]
     for before in range(cuts - 1):
         @pl.when(cut > before)
         def _():
+            for side in range(3):
+                @on_side(side)
+                def _():
+                    await_coarse(side, before * lc + 1, lc, before + 1)
             state = [ybuf[m] for m in range(2)]
             for n in range(lc):
                 slice_no = before * lc + n
                 out = coarse_step(state, amps_at(slice_no, 0))
-                await_coarse(1, slice_no + 1)
-                for side in (0, 2):
-                    @on_side(side)
-                    def _():
-                        await_coarse(side, slice_no + 1)
                 state = following(out, slice_no + 1)
             for m in range(2):
                 ybuf[m] = state[m]
 
-    for n in range(lc - 1):
-        for side in (0, 2):
-            @on_side(side)
-            def _():
-                await_coarse(side, base + n + 1)
+    for side in (0, 2):
+        @on_side(side)
+        def _():
+            await_coarse(side, base + 1, lc, cut + 1)
     state = [ybuf[m] for m in range(2)]
     for n in range(lc):
         out = coarse_step(state, amps[n][0])
@@ -457,9 +465,8 @@
 
     @pl.when(cut == 0)
     def _():
-        each_coarse_send(0, lc, True, lambda copy: copy.wait_send())
-    for n in range(lc):
-        each_coarse_send(base + n + 1, n, n < lc - 1, lambda copy: copy.wait_send())
+        each_coarse_send(0, 1, 0, 0, lambda copy: copy.wait_send())
+    each_coarse_send(base + 1, lc, cut + 1, 1, lambda copy: copy.wait_send())
 
 
 def finish(fine_ref, new_ref, pbuf, spread_ref, ends_out, new_out, total, sems):
@@ -520,11 +527,11 @@
                 pltpu.VMEM((slices + 1, 2, 3 * crow, ccol), F32),
                 pltpu.VMEM((4 * rows, ccol), F32),
                 pltpu.VMEM((2, 3 * crow, ccol), F32),
-                pltpu.SemaphoreType.DMA((6,)),
+                pltpu.SemaphoreType.DMA((8,)),
                 pltpu.SemaphoreType.DMA((3, 2)),
                 pltpu.SemaphoreType.DMA((3, 2)),
-                pltpu.SemaphoreType.DMA((cuts, 3, lc + 1)),
-                pltpu.SemaphoreType.DMA((3, slices + 1)),
+                pltpu.SemaphoreType.DMA((cuts, 3, 2)),
+                pltpu.SemaphoreType.DMA((3, cuts + 1)),
             ],
             compiler_params=pltpu.CompilerParams(
                 collective_id=0, has_side_effects=True, vmem_limit_bytes=32 * 1024 * 1024

time: 12.8 us -> 12.9 us (level)
  the two profiles are of different devices: /device:TPU:1 before, /device:TPU:15 now
where the time goes in v4:
time: 12.9 us; the launch traced here: 12.7 us
  Pallas kernels  12.1 us (94%)
  between operations  0.64 us (5%)
    pallas_call x1, Pallas kernels, local(): pl.pallas_call(functools.partial(kernel, sizes), out_shape=(jax.ShapeDtyp...  11.1 us
    pallas_call x1, Pallas kernels, local(): pl.pallas_call(finish, out_shape=(jax.ShapeDtypeStruct(starts.shape, F32)...  1.03 us

profile of v4, /device:TPU:15, one launch (start us, length us, event | category | flops | bytes accessed | tf_op | source)
XLA Modules:
  0.0 12.7 jit_solution(4646800191075949333)
XLA Ops:
  0.6 11.1 %shard_map.77 = (f32[4,2,32,512]{3,2,1,0:T(8,128)S(1)}, f32[4,2,8,128]{3,2,1,0:T(8,128)S(1)}, f32[4,64,128]{2,1,0:T(8,128)S(1)}, bf16[256,512]{1,0:T(8,128)(2,1)S(1)}) custom-call(f32[4,2,32,512]{3,2,1,0:T(8,128)} %starts_hbm.1, f32[4,2,8,128]{3,2,1,0:T(8,128)} %prev_hbm.1, s32[32,512]{1,0:T(8,128)} %zone_hbm.1, f32[4,8]{1,0:T(4,128)} %mat_hbm.1, ...), custom_call_target="tpu_custom_call" | custom-call | tf_op jit(solution)/shard_map/pallas_call | solution.py:497
  11.7 1.0 %shard_map.78 = (f32[4,2,32,512]{3,2,1,0:T(8,128)}, f32[4,2,8,128]{3,2,1,0:T(8,128)}) custom-call(f32[4,2,32,512]{3,2,1,0:T(8,128)S(1)} %get-tuple-element.6.fine_ref, f32[4,2,8,128]{3,2,1,0:T(8,128)S(1)} %get-tuple-element.7.new_ref, f32[4,64,128]{2,1,0:T(8,128)S(1)} %get-tuple-element.8.pbuf, bf16[256,512]{1,0:T(8,128)(2,1)S(1)} %get-tuple-element.9.spread_ref), custom_call_target="tpu_custom_call" | custom-call | tf_op jit(solution)/shard_map/pallas_call | solution.py:543

commit v5 on v3

--- a/solution.py
+++ b/solution.py
@@ -146,6 +146,73 @@
             md[m, n : n + 1, :] = s0[n, m, rows + 7 : rows + 8, :]
             md[m, half + n : half + n + 1, :] = s0[n, m, rows + 6 : rows + 7, :]
 
+    def lateral(value, edge, col):
+        width = value.shape[1]
+        left = jnp.where(col == 0, edge, pltpu.roll(value, 1, 1))
+        right = jnp.where(col == width - 1, edge, pltpu.roll(value, width - 1, 1))
+        return 0.5 * (value + left), 0.5 * (value + right)
+
+    def five(center, up, down, edge, col):
+        west, east = lateral(center, edge, col)
+        north = 0.5 * (center + up)
+        south = 0.5 * (center + down)
+        width = center.shape[1]
+        return (
+            jnp.where(col == width - 1, 0.0, east),
+            jnp.where(col == 0, 0.0, west),
+            north,
+            south,
+            (west + east) + (north + south),
+        )
+
+    def make_weights(i):
+        low = 8 + 8 * i
+        for m in range(2):
+            made = five(
+                rf[m, low : low + 8, :], rf[m, low - 1 : low + 7, :],
+                rf[m, low + 1 : low + 9, :], mat_ref[m, 0], col8,
+            )
+            for k in range(5):
+                wt[m, k, 8 * i : 8 * i + 8, :] = made[k]
+
+    def spread_sum(weights, center, up, down):
+        width = center.shape[1]
+        east, west, north, south, whole = weights
+        total = east * pltpu.roll(center, width - 1, 1) + west * pltpu.roll(center, 1, 1)
+        return (total + (north * up + south * down)) - whole * center
+
+    def amps_at(slice_no, offset):
+        return current_ref[bounds_ref[slice_no] + offset].astype(F32) * 0.001
+
+    amps = [[amps_at(base + n, j) for j in range(2)] for n in range(lc)]
+
+    def fine_chunk(source, n, i, amperes):
+        low = 8 + 8 * i
+        at = slice(8 * i, 8 * i + 8)
+        sums = []
+        for m in range(2):
+            center = source[n, m, low : low + 8, :]
+            weights = [wt[m, k, at, :] for k in range(5)]
+            sums.append((center, spread_sum(
+                weights, center, source[n, m, low - 1 : low + 7, :],
+                source[n, m, low + 1 : low + 9, :],
+            )))
+        return advance(sums, pqs[2, at, :] * amperes, pqs[0, at, :], pqs[1, at, :])
+
+    def first_step(n, i):
+        out = fine_chunk(s0, n, i, amps[n][0])
+        for m in range(2):
+            s1[n, m, 8 + 8 * i : 16 + 8 * i, :] = out[m]
+
+    for i in range(1, chunks - 1):
+        make_weights(i)
+    for n in range(lc):
+        for i in range(1, chunks - 1):
+            first_step(n, i)
+
+    own_c = restricted(fl[...].reshape(4 * rows, cols), tbuf)
+    for m in range(4):
+        cf[m, crow : 2 * crow, :] = own_c[m * crow : (m + 1) * crow]
     ups = jnp.where(has_up, 1, 0) + jnp.where(has_down, 1, 0)
     pl.semaphore_wait(barrier, ups + (cuts - 1) * (1 + ups))
 
@@ -168,36 +235,35 @@
             device_id_type=MESH,
         )
 
-    def coarse_copy(side, g, local_no, dest):
+    def coarse_copy(side, first, count, mark, kind, dest):
         return pltpu.make_async_remote_copy(
-            src_ref=grid_c.at[g, :, pl.ds(crow, crow), :],
-            dst_ref=grid_c.at[g, :, pl.ds((2 - side) * crow, crow), :],
-            send_sem=send_c.at[dest, side, local_no],
-            recv_sem=recv_c.at[2 - side, g],
+            src_ref=grid_c.at[pl.ds(first, count), :, pl.ds(crow, crow), :],
+            dst_ref=grid_c.at[pl.ds(first, count), :, pl.ds((2 - side) * crow, crow), :],
+            send_sem=send_c.at[dest, side, kind],
+            recv_sem=recv_c.at[2 - side, mark],
             device_id=where_is(side, None if dest == 0 else dest),
             device_id_type=MESH,
         )
 
-    def each_coarse_send(g, local_no, nearby, action):
+    def each_coarse_send(first, count, mark, kind, action):
+        for side in (0, 2):
+            @on_side(side)
+            def _():
+                action(coarse_copy(side, first, count, mark, kind, 0))
         for dest in range(1, cuts):
             @pl.when(cut < dest)
             def _():
                 for side in (1, 0, 2):
                     @on_side(side)
                     def _():
-                        action(coarse_copy(side, g, local_no, dest))
-        if nearby:
-            for side in (0, 2):
-                @on_side(side)
-                def _():
-                    action(coarse_copy(side, g, local_no, 0))
-
-    def await_coarse(side, g):
+                        action(coarse_copy(side, first, count, mark, kind, dest))
+
+    def await_coarse(side, first, count, mark):
         pltpu.make_async_remote_copy(
-            src_ref=grid_c.at[g, :, pl.ds(crow, crow), :],
-            dst_ref=grid_c.at[g, :, pl.ds(side * crow, crow), :],
+            src_ref=grid_c.at[pl.ds(first, count), :, pl.ds(crow, crow), :],
+            dst_ref=grid_c.at[pl.ds(first, count), :, pl.ds(side * crow, crow), :],
             send_sem=send_c.at[0, 0, 0],
-            recv_sem=recv_c.at[side, g],
+            recv_sem=recv_c.at[side, mark],
             device_id=where_is(1, lax.rem(cut + 1, cuts)),
             device_id_type=MESH,
         ).wait_recv()
@@ -224,9 +290,6 @@
             cf[m, 2 * crow : 3 * crow, :] = jnp.full((crow, ccol), mat_ref[m, 0], F32)
         grid_c[:, :, 2 * crow : 3 * crow, :] = jnp.zeros(grid_c.shape[:2] + (crow, ccol), F32)
 
-    own_c = restricted(fl[...].reshape(4 * rows, cols), tbuf)
-    for m in range(4):
-        cf[m, crow : 2 * crow, :] = own_c[m * crow : (m + 1) * crow]
     for side in (0, 2):
         @on_side(side)
         def _():
@@ -237,71 +300,7 @@
         first = restricted(s0[0, :, 8 : 8 + rows, :].reshape(2 * rows, cols), tbuf)
         for m in range(2):
             grid_c[0, m, crow : 2 * crow, :] = first[m * crow : (m + 1) * crow]
-        each_coarse_send(0, lc, True, lambda copy: copy.start())
-
-    def lateral(value, edge, col):
-        width = value.shape[1]
-        left = jnp.where(col == 0, edge, pltpu.roll(value, 1, 1))
-        right = jnp.where(col == width - 1, edge, pltpu.roll(value, width - 1, 1))
-        return 0.5 * (value + left), 0.5 * (value + right)
-
-    def five(center, up, down, edge, col):
-        west, east = lateral(center, edge, col)
-        north = 0.5 * (center + up)
-        south = 0.5 * (center + down)
-        width = center.shape[1]
-        return (
-            jnp.where(col == width - 1, 0.0, east),
-            jnp.where(col == 0, 0.0, west),
-            north,
-            south,
-            (west + east) + (north + south),
-        )
-
-    def make_weights(i):
-        low = 8 + 8 * i
-        for m in range(2):
-            made = five(
-                rf[m, low : low + 8, :], rf[m, low - 1 : low + 7, :],
-                rf[m, low + 1 : low + 9, :], mat_ref[m, 0], col8,
-            )
-            for k in range(5):
-                wt[m, k, 8 * i : 8 * i + 8, :] = made[k]
-
-    def spread_sum(weights, center, up, down):
-        width = center.shape[1]
-        east, west, north, south, whole = weights
-        total = east * pltpu.roll(center, width - 1, 1) + west * pltpu.roll(center, 1, 1)
-        return (total + (north * up + south * down)) - whole * center
-
-    def amps_at(slice_no, offset):
-        return current_ref[bounds_ref[slice_no] + offset].astype(F32) * 0.001
-
-    amps = [[amps_at(base + n, j) for j in range(2)] for n in range(lc)]
-
-    def fine_chunk(source, n, i, amperes):
-        low = 8 + 8 * i
-        at = slice(8 * i, 8 * i + 8)
-        sums = []
-        for m in range(2):
-            center = source[n, m, low : low + 8, :]
-            weights = [wt[m, k, at, :] for k in range(5)]
-            sums.append((center, spread_sum(
-                weights, center, source[n, m, low - 1 : low + 7, :],
-                source[n, m, low + 1 : low + 9, :],
-            )))
-        return advance(sums, pqs[2, at, :] * amperes, pqs[0, at, :], pqs[1, at, :])
-
-    def first_step(n, i):
-        out = fine_chunk(s0, n, i, amps[n][0])
-        for m in range(2):
-            s1[n, m, 8 + 8 * i : 16 + 8 * i, :] = out[m]
-
-    for i in range(1, chunks - 1):
-        make_weights(i)
-    for n in range(lc):
-        for i in range(1, chunks - 1):
-            first_step(n, i)
+        each_coarse_send(0, 1, 0, 0, lambda copy: copy.start())
 
     for side in (0, 2):
         @on_side(side)
@@ -371,7 +370,7 @@
             grid_c[base + n + 1, m, crow : 2 * crow, :] = (
                 mean[m * crow : (m + 1) * crow] - prev_ref[n, m]
             )
-        each_coarse_send(base + n + 1, n, n < lc - 1, lambda copy: copy.start())
+    each_coarse_send(base + 1, lc, cut + 1, 1, lambda copy: copy.start())
 
     for side in (0, 2):
         @on_side(side)
@@ -409,34 +408,32 @@
 
     @pl.when(cut > 0)
     def _():
-        await_coarse(1, 0)
-    for side in (0, 2):
-        @on_side(side)
-        def _():
-            await_coarse(side, 0)
+        await_coarse(1, 0, 1, 0)
+    for side in (0, 2):
+        @on_side(side)
+        def _():
+            await_coarse(side, 0, 1, 0)
     for m in range(2):
         ybuf[m] = grid_c[0, m]
     for before in range(cuts - 1):
         @pl.when(cut > before)
         def _():
+            for side in range(3):
+                @on_side(side)
+                def _():
+                    await_coarse(side, before * lc + 1, lc, before + 1)
             state = [ybuf[m] for m in range(2)]
             for n in range(lc):
                 slice_no = before * lc + n
                 out = coarse_step(state, amps_at(slice_no, 0))
-                await_coarse(1, slice_no + 1)
-                for side in (0, 2):
-                    @on_side(side)
-                    def _():
-                        await_coarse(side, slice_no + 1)
                 state = following(out, slice_no + 1)
             for m in range(2):
                 ybuf[m] = state[m]
 
-    for n in range(lc - 1):
-        for side in (0, 2):
-            @on_side(side)
-            def _():
-                await_coarse(side, base + n + 1)
+    for side in (0, 2):
+        @on_side(side)
+        def _():
+            await_coarse(side, base + 1, lc, cut + 1)
     state = [ybuf[m] for m in range(2)]
     for n in range(lc):
         out = coarse_step(state, amps[n][0])
@@ -457,9 +454,8 @@
 
     @pl.when(cut == 0)
     def _():
-        each_coarse_send(0, lc, True, lambda copy: copy.wait_send())
-    for n in range(lc):
-        each_coarse_send(base + n + 1, n, n < lc - 1, lambda copy: copy.wait_send())
+        each_coarse_send(0, 1, 0, 0, lambda copy: copy.wait_send())
+    each_coarse_send(base + 1, lc, cut + 1, 1, lambda copy: copy.wait_send())
 
 
 def finish(fine_ref, new_ref, pbuf, spread_ref, ends_out, new_out, total, sems):
@@ -523,8 +519,8 @@
                 pltpu.SemaphoreType.DMA((6,)),
                 pltpu.SemaphoreType.DMA((3, 2)),
                 pltpu.SemaphoreType.DMA((3, 2)),
-                pltpu.SemaphoreType.DMA((cuts, 3, lc + 1)),
-                pltpu.SemaphoreType.DMA((3, slices + 1)),
+                pltpu.SemaphoreType.DMA((cuts, 3, 2)),
+                pltpu.SemaphoreType.DMA((3, cuts + 1)),
             ],
             compiler_params=pltpu.CompilerParams(
                 collective_id=0, has_side_effects=True, vmem_limit_bytes=32 * 1024 * 1024

time: 12.8 us -> 12.6 us (0.984)
  the two profiles are of different devices: /device:TPU:1 before, /device:TPU:15 now
where the time goes in v5:
time: 12.6 us; the launch traced here: 12.5 us
  Pallas kernels  11.9 us (94%)
  between operations  0.64 us (5%)
    pallas_call x1, Pallas kernels, local(): pl.pallas_call(functools.partial(kernel, sizes), out_shape=(jax.ShapeDtyp...  10.8 us
    pallas_call x1, Pallas kernels, local(): pl.pallas_call(finish, out_shape=(jax.ShapeDtypeStruct(starts.shape, F32)...  1.03 us

profile of v5, /device:TPU:15, one launch (start us, length us, event | category | flops | bytes accessed | tf_op | source)
XLA Modules:
  0.0 12.5 jit_solution(4198160355518798736)
XLA Ops:
  0.6 10.8 %shard_map.77 = (f32[4,2,32,512]{3,2,1,0:T(8,128)S(1)}, f32[4,2,8,128]{3,2,1,0:T(8,128)S(1)}, f32[4,64,128]{2,1,0:T(8,128)S(1)}, bf16[256,512]{1,0:T(8,128)(2,1)S(1)}) custom-call(f32[4,2,32,512]{3,2,1,0:T(8,128)} %starts_hbm.1, f32[4,2,8,128]{3,2,1,0:T(8,128)} %prev_hbm.1, s32[32,512]{1,0:T(8,128)} %zone_hbm.1, f32[4,8]{1,0:T(4,128)} %mat_hbm.1, ...), custom_call_target="tpu_custom_call" | custom-call | tf_op jit(solution)/shard_map/pallas_call | solution.py:486
  11.5 1.0 %shard_map.78 = (f32[4,2,32,512]{3,2,1,0:T(8,128)}, f32[4,2,8,128]{3,2,1,0:T(8,128)}) custom-call(f32[4,2,32,512]{3,2,1,0:T(8,128)S(1)} %get-tuple-element.6.fine_ref, f32[4,2,8,128]{3,2,1,0:T(8,128)S(1)} %get-tuple-element.7.new_ref, f32[4,64,128]{2,1,0:T(8,128)S(1)} %get-tuple-element.8.pbuf, bf16[256,512]{1,0:T(8,128)(2,1)S(1)} %get-tuple-element.9.spread_ref), custom_call_target="tpu_custom_call" | custom-call | tf_op jit(solution)/shard_map/pallas_call | solution.py:532

commit v6 on v5

--- a/solution.py
+++ b/solution.py
@@ -200,13 +200,14 @@
         return advance(sums, pqs[2, at, :] * amperes, pqs[0, at, :], pqs[1, at, :])
 
     def first_step(n, i):
-        out = fine_chunk(s0, n, i, amps[n][0])
+        out = fine_chunk(s0, n, i, amps_at(base + n, 0))
         for m in range(2):
             s1[n, m, 8 + 8 * i : 16 + 8 * i, :] = out[m]
 
     for i in range(1, chunks - 1):
         make_weights(i)
-    for n in range(lc):
+    @pl.loop(0, lc)
+    def _(n):
         for i in range(1, chunks - 1):
             first_step(n, i)
 
@@ -358,11 +359,12 @@
             s1[n, m, rows + 8 : rows + 9, :] = kept[half + n : half + n + 1]
 
     load_prev.wait()
-    for n in range(lc):
+    @pl.loop(0, lc)
+    def _(n):
         for i in (0, chunks - 1):
             first_step(n, i)
         for i in range(chunks):
-            out = fine_chunk(s1, n, i, amps[n][1])
+            out = fine_chunk(s1, n, i, amps_at(base + n, 1))
             for m in range(2):
                 ends_ref[n, m, 8 * i : 8 * i + 8, :] = out[m]
         mean = restricted(ends_ref[n].reshape(2 * rows, cols), tbuf)

time: 12.6 us -> 13.4 us (1.063)
  Pallas kernels: 11.9 us -> 12.6 us
    pallas_call x1, Pallas kernels: 10.8 us -> 11.5 us  [local(): pl.pallas_call(functools.partial(kernel, sizes), out_shape=(jax.ShapeDtyp...]
where the time goes in v6:
time: 13.4 us; the launch traced here: 13.2 us
  Pallas kernels  12.6 us (94%)
  between operations  0.64 us (5%)
    pallas_call x1, Pallas kernels, local(): pl.pallas_call(functools.partial(kernel, sizes), out_shape=(jax.ShapeDtyp...  11.5 us
    pallas_call x1, Pallas kernels, local(): pl.pallas_call(finish, out_shape=(jax.ShapeDtypeStruct(starts.shape, F32)...  1.03 us

profile of v6, /device:TPU:15, one launch (start us, length us, event | category | flops | bytes accessed | tf_op | source)
XLA Modules:
  0.0 13.2 jit_solution(9309308515040188671)
XLA Ops:
  0.6 11.5 %shard_map.77 = (f32[4,2,32,512]{3,2,1,0:T(8,128)S(1)}, f32[4,2,8,128]{3,2,1,0:T(8,128)S(1)}, f32[4,64,128]{2,1,0:T(8,128)S(1)}, bf16[256,512]{1,0:T(8,128)(2,1)S(1)}) custom-call(f32[4,2,32,512]{3,2,1,0:T(8,128)} %starts_hbm.1, f32[4,2,8,128]{3,2,1,0:T(8,128)} %prev_hbm.1, s32[32,512]{1,0:T(8,128)} %zone_hbm.1, f32[4,8]{1,0:T(4,128)} %mat_hbm.1, ...), custom_call_target="tpu_custom_call" | custom-call | tf_op jit(solution)/shard_map/pallas_call | solution.py:488
  12.2 1.0 %shard_map.78 = (f32[4,2,32,512]{3,2,1,0:T(8,128)}, f32[4,2,8,128]{3,2,1,0:T(8,128)}) custom-call(f32[4,2,32,512]{3,2,1,0:T(8,128)S(1)} %get-tuple-element.6.fine_ref, f32[4,2,8,128]{3,2,1,0:T(8,128)S(1)} %get-tuple-element.7.new_ref, f32[4,64,128]{2,1,0:T(8,128)S(1)} %get-tuple-element.8.pbuf, bf16[256,512]{1,0:T(8,128)(2,1)S(1)} %get-tuple-element.9.spread_ref), custom_call_target="tpu_custom_call" | custom-call | tf_op jit(solution)/shard_map/pallas_call | solution.py:534

commit v7 on v3

--- a/solution.py
+++ b/solution.py
@@ -168,36 +168,35 @@
             device_id_type=MESH,
         )
 
-    def coarse_copy(side, g, local_no, dest):
+    def coarse_copy(side, first, count, mark, kind, dest):
         return pltpu.make_async_remote_copy(
-            src_ref=grid_c.at[g, :, pl.ds(crow, crow), :],
-            dst_ref=grid_c.at[g, :, pl.ds((2 - side) * crow, crow), :],
-            send_sem=send_c.at[dest, side, local_no],
-            recv_sem=recv_c.at[2 - side, g],
+            src_ref=grid_c.at[pl.ds(first, count), :, pl.ds(crow, crow), :],
+            dst_ref=grid_c.at[pl.ds(first, count), :, pl.ds((2 - side) * crow, crow), :],
+            send_sem=send_c.at[dest, side, kind],
+            recv_sem=recv_c.at[2 - side, mark],
             device_id=where_is(side, None if dest == 0 else dest),
             device_id_type=MESH,
         )
 
-    def each_coarse_send(g, local_no, nearby, action):
+    def each_coarse_send(first, count, mark, kind, action):
+        for side in (0, 2):
+            @on_side(side)
+            def _():
+                action(coarse_copy(side, first, count, mark, kind, 0))
         for dest in range(1, cuts):
             @pl.when(cut < dest)
             def _():
                 for side in (1, 0, 2):
                     @on_side(side)
                     def _():
-                        action(coarse_copy(side, g, local_no, dest))
-        if nearby:
-            for side in (0, 2):
-                @on_side(side)
-                def _():
-                    action(coarse_copy(side, g, local_no, 0))
-
-    def await_coarse(side, g):
+                        action(coarse_copy(side, first, count, mark, kind, dest))
+
+    def await_coarse(side, first, count, mark):
         pltpu.make_async_remote_copy(
-            src_ref=grid_c.at[g, :, pl.ds(crow, crow), :],
-            dst_ref=grid_c.at[g, :, pl.ds(side * crow, crow), :],
+            src_ref=grid_c.at[pl.ds(first, count), :, pl.ds(crow, crow), :],
+            dst_ref=grid_c.at[pl.ds(first, count), :, pl.ds(side * crow, crow), :],
             send_sem=send_c.at[0, 0, 0],
-            recv_sem=recv_c.at[side, g],
+            recv_sem=recv_c.at[side, mark],
             device_id=where_is(1, lax.rem(cut + 1, cuts)),
             device_id_type=MESH,
         ).wait_recv()
@@ -237,7 +236,7 @@
         first = restricted(s0[0, :, 8 : 8 + rows, :].reshape(2 * rows, cols), tbuf)
         for m in range(2):
             grid_c[0, m, crow : 2 * crow, :] = first[m * crow : (m + 1) * crow]
-        each_coarse_send(0, lc, True, lambda copy: copy.start())
+        each_coarse_send(0, 1, 0, 0, lambda copy: copy.start())
 
     def lateral(value, edge, col):
         width = value.shape[1]
@@ -371,7 +370,7 @@
             grid_c[base + n + 1, m, crow : 2 * crow, :] = (
                 mean[m * crow : (m + 1) * crow] - prev_ref[n, m]
             )
-        each_coarse_send(base + n + 1, n, n < lc - 1, lambda copy: copy.start())
+    each_coarse_send(base + 1, lc, cut + 1, 1, lambda copy: copy.start())
 
     for side in (0, 2):
         @on_side(side)
@@ -409,34 +408,32 @@
 
     @pl.when(cut > 0)
     def _():
-        await_coarse(1, 0)
-    for side in (0, 2):
-        @on_side(side)
-        def _():
-            await_coarse(side, 0)
+        await_coarse(1, 0, 1, 0)
+    for side in (0, 2):
+        @on_side(side)
+        def _():
+            await_coarse(side, 0, 1, 0)
     for m in range(2):
         ybuf[m] = grid_c[0, m]
     for before in range(cuts - 1):
         @pl.when(cut > before)
         def _():
+            for side in range(3):
+                @on_side(side)
+                def _():
+                    await_coarse(side, before * lc + 1, lc, before + 1)
             state = [ybuf[m] for m in range(2)]
             for n in range(lc):
                 slice_no = before * lc + n
                 out = coarse_step(state, amps_at(slice_no, 0))
-                await_coarse(1, slice_no + 1)
-                for side in (0, 2):
-                    @on_side(side)
-                    def _():
-                        await_coarse(side, slice_no + 1)
                 state = following(out, slice_no + 1)
             for m in range(2):
                 ybuf[m] = state[m]
 
-    for n in range(lc - 1):
-        for side in (0, 2):
-            @on_side(side)
-            def _():
-                await_coarse(side, base + n + 1)
+    for side in (0, 2):
+        @on_side(side)
+        def _():
+            await_coarse(side, base + 1, lc, cut + 1)
     state = [ybuf[m] for m in range(2)]
     for n in range(lc):
         out = coarse_step(state, amps[n][0])
@@ -457,9 +454,8 @@
 
     @pl.when(cut == 0)
     def _():
-        each_coarse_send(0, lc, True, lambda copy: copy.wait_send())
-    for n in range(lc):
-        each_coarse_send(base + n + 1, n, n < lc - 1, lambda copy: copy.wait_send())
+        each_coarse_send(0, 1, 0, 0, lambda copy: copy.wait_send())
+    each_coarse_send(base + 1, lc, cut + 1, 1, lambda copy: copy.wait_send())
 
 
 def finish(fine_ref, new_ref, pbuf, spread_ref, ends_out, new_out, total, sems):
@@ -523,8 +519,8 @@
                 pltpu.SemaphoreType.DMA((6,)),
                 pltpu.SemaphoreType.DMA((3, 2)),
                 pltpu.SemaphoreType.DMA((3, 2)),
-                pltpu.SemaphoreType.DMA((cuts, 3, lc + 1)),
-                pltpu.SemaphoreType.DMA((3, slices + 1)),
+                pltpu.SemaphoreType.DMA((cuts, 3, 2)),
+                pltpu.SemaphoreType.DMA((3, cuts + 1)),
             ],
             compiler_params=pltpu.CompilerParams(
                 collective_id=0, has_side_effects=True, vmem_limit_bytes=32 * 1024 * 1024

time: 12.8 us -> 12.6 us (0.984)
  the two profiles are of different devices: /device:TPU:1 before, /device:TPU:15 now
where the time goes in v7:
time: 12.6 us; the launch traced here: 12.5 us
  Pallas kernels  11.9 us (94%)
  between operations  0.64 us (5%)
    pallas_call x1, Pallas kernels, local(): pl.pallas_call(functools.partial(kernel, sizes), out_shape=(jax.ShapeDtyp...  10.8 us
    pallas_call x1, Pallas kernels, local(): pl.pallas_call(finish, out_shape=(jax.ShapeDtypeStruct(starts.shape, F32)...  1.03 us

profile of v7, /device:TPU:15, one launch (start us, length us, event | category | flops | bytes accessed | tf_op | source)
XLA Modules:
  0.0 12.5 jit_solution(14885364304580970507)
XLA Ops:
  0.6 10.8 %shard_map.77 = (f32[4,2,32,512]{3,2,1,0:T(8,128)S(1)}, f32[4,2,8,128]{3,2,1,0:T(8,128)S(1)}, f32[4,64,128]{2,1,0:T(8,128)S(1)}, bf16[256,512]{1,0:T(8,128)(2,1)S(1)}) custom-call(f32[4,2,32,512]{3,2,1,0:T(8,128)} %starts_hbm.1, f32[4,2,8,128]{3,2,1,0:T(8,128)} %prev_hbm.1, s32[32,512]{1,0:T(8,128)} %zone_hbm.1, f32[4,8]{1,0:T(4,128)} %mat_hbm.1, ...), custom_call_target="tpu_custom_call" | custom-call | tf_op jit(solution)/shard_map/pallas_call | solution.py:486
  11.5 1.0 %shard_map.78 = (f32[4,2,32,512]{3,2,1,0:T(8,128)}, f32[4,2,8,128]{3,2,1,0:T(8,128)}) custom-call(f32[4,2,32,512]{3,2,1,0:T(8,128)S(1)} %get-tuple-element.6.fine_ref, f32[4,2,8,128]{3,2,1,0:T(8,128)S(1)} %get-tuple-element.7.new_ref, f32[4,64,128]{2,1,0:T(8,128)S(1)} %get-tuple-element.8.pbuf, bf16[256,512]{1,0:T(8,128)(2,1)S(1)} %get-tuple-element.9.spread_ref), custom_call_target="tpu_custom_call" | custom-call | tf_op jit(solution)/shard_map/pallas_call | solution.py:532
